TPU v7x, 256 devices: a whole 4x4x8 slice. The times are simulated.
256 devices in a mesh: dp: 64 (over z, y, core), group: 4 (over x).
Axes of the slice: x: 4, y: 4, z: 8, core: 2. Of those that a mesh axis runs over, the one named last changes fastest.
Arguments:
- acts: bfloat16 [32768, 2048], P('dp'), may hold values from -6 to 6
- grad_out: bfloat16 [32768, 8192], P('dp', 'group'), may hold values from -700 to 700
- projector: bfloat16 [2048, 256], P('dp'), may hold values from -0.125 to 0.125
- moment_one: float32 [256, 8192], P(None, 'group'), may hold values from -6 to 6
- moment_two: float32 [256, 8192], P(None, 'group'), may hold values from 0.25 to 4
Outputs:
- update: float32 [2048, 8192], P('dp', 'group')
- moment_one_new: float32 [256, 8192], P(None, 'group')
- moment_two_new: float32 [256, 8192], P(None, 'group')
All inputs are finite; a program needn't handle non-finite values.
Results may differ from a plain program's by a relative error of at most 0.00035.
Values may be sent and summed in bfloat16 or wider, within the bound.
A program may use at most 128 MiB of HBM per device.

v0:
```python
import jax
import jax.numpy as jnp
from jax import lax
from jax.sharding import PartitionSpec as P

beta_one = 0.9
beta_two = 0.95
bias_one = 1.0 - 0.9**10
bias_two = 1.0 - 0.95**10
galore_scale = 0.25


def adam_moments(proj, first_old, second_old, energy, entries):
    clip = jnp.minimum(1.0, 1.0 / jnp.sqrt(energy / entries + 1e-06))
    clipped = clip * proj
    first = beta_one * first_old + (1.0 - beta_one) * clipped
    second = beta_two * second_old + (1.0 - beta_two) * clipped * clipped
    return (first, second)


def on_device(acts, grad_out, projector, moment_one, moment_two):
    rank = projector.shape[1]
    entries = float(rank * grad_out.shape[1] * lax.axis_size("group"))
    grad_rows = lax.psum_scatter(
        lax.dot_general(
            acts, grad_out, (((0,), (0,)), ((), ())), preferred_element_type=jnp.float32
        ),
        "dp",
        scatter_dimension=0,
        tiled=True,
    )
    partial_value = jnp.dot(
        projector.astype(jnp.float32).T, grad_rows, precision=lax.Precision.HIGHEST
    )
    proj = lax.psum(partial_value, "dp")
    energy = lax.psum(jnp.sum(proj * proj), "group")
    first, second = adam_moments(proj, moment_one, moment_two, energy, entries)
    direction = first / bias_one / (jnp.sqrt(second / bias_two) + 1e-08)
    update = galore_scale * jnp.dot(
        projector.astype(jnp.float32), direction, precision=lax.Precision.HIGHEST
    )
    return (update, first, second)


def solution(mesh):
    placed = (P("dp", None), P("dp", "group"), P("dp", None), P(None, "group"), P(None, "group"))
    return jax.shard_map(
        on_device,
        mesh=mesh,
        in_specs=placed,
        out_specs=(P("dp", "group"), P(None, "group"), P(None, "group")),
        check_vma=False,
    )
```

profile of v0, /device:TPU:1, one launch (start us, length us, event | category | flops | bytes accessed | tf_op | source)
XLA Modules:
  0.0 440.4 jit_solution(2699538560838941993)
XLA Ops:
  7.2 0.0 copy-start
  7.2 0.0 reduce-scatter.2.cloned.1.call-start
  7.2 1.5 copy-done
  8.8 9.7 %fusion.8 = f32[2048,2048]{1,0:T(8,128)} fusion(bf16[512,2048]{1,0:T(8,128)(2,1)S(1)} %copy-done, bf16[512,2048]{1,0:T(8,128)(2,1)} %param.6), kind=kOutput, calls=%fused_computation.14 | convolution fusion | flops 4294967296 | bytes 20971520 | tf_op jit(solution)/shard_map/dot_general | solution.py:25
  18.5 0.0 copy-start.1
  18.5 0.0 reduce-scatter.2.cloned.1.call-update
  18.5 0.0 all-reduce.2.cloned.1.call-start
  18.5 189.1 %reduce-scatter.2.cloned.1.call-done = f32[32,2048]{1,0:T(8,128)} async-done(((f32[2048,2048]{1,0:T(8,128)}), f32[32,2048]{1,0:T(8,128)}) %reduce-scatter.2.cloned.1.call-update) | async-done | bytes 262160 | tf_op jit(solution)/shard_map/reduce_scatter | solution.py:24
  207.7 0.0 copy-done.1
  207.7 3.3 convolution_bitcast_fusion
  211.0 0.0 all-reduce.2.cloned.1.call-update
  211.0 2.9 copy.8
  213.9 188.1 %all-reduce.2.cloned.1.call-done = f32[256,2048]{0,1:T(8,128)} async-done(((f32[256,2048]{0,1:T(8,128)}), f32[256,2048]{0,1:T(8,128)}) %all-reduce.2.cloned.1.call-update) | async-done | bytes 2097168 | tf_op jit(solution)/shard_map/psum | solution.py:35
  402.0 2.7 multiply_reduce_fusion
  404.7 2.9 copy.9
  407.6 9.0 %psum.15 = f32[]{:T(128)} all-reduce(f32[]{:T(128)} %multiply_reduce_fusion), channel_id=1, replica_groups=mesh['dp'=64,'group'=4] {'group'}, use_global_device_ids=true, to_apply=%region_3.0 | all-reduce | flops 1 | bytes 8 | tf_op jit(solution)/shard_map/psum | solution.py:36
  417.3 5.5 %multiply_add_fusion = (f32[256,2048]{0,1:T(8,128)}, f32[256,2048]{0,1:T(8,128)}) fusion(f32[256,2048]{0,1:T(8,128)} %copy.8, f32[256,2048]{0,1:T(8,128)} %all-reduce.2.cloned.1.call-done, f32[]{:T(128)S(6)} %min.3, f32[256,2048]{0,1:T(8,128)} %copy.9), kind=kLoop, calls=%fused_computation.6 | loop fusion | flops 4194304 | bytes 10485764 | tf_op jit(solution)/shard_map/add | solution.py:16
  422.7 2.9 copy.10
  425.6 5.0 %fusion = f32[32,2048]{1,0:T(8,128)} fusion(bf16[32,256]{1,0:T(8,128)(2,1)S(1)} %copy-done.1, f32[256,2048]{0,1:T(8,128)} %get-tuple-element.7, f32[256,2048]{0,1:T(8,128)} %get-tuple-element.6), kind=kOutput, calls=%fused_computation.3 | convolution fusion | flops 203489280 | bytes 4472832 | tf_op jit(solution)/shard_map/dot_general | solution.py:39
  430.7 2.9 copy.11
Async XLA Ops:
  7.2 1.6 copy-start
  7.2 200.5 %reduce-scatter.2.cloned.1.call-start = ((), (), s32[]{:S(2)}) async-start(), calls=%async_computation.1 | async-start | bytes 17039360 | tf_op jit(solution)/shard_map/reduce_scatter | solution.py:24
  18.5 189.2 %copy-start.1 = (bf16[32,256]{1,0:T(8,128)(2,1)S(1)}, bf16[32,256]{1,0:T(8,128)(2,1)}, u32[]{:S(2)}) copy-start(bf16[32,256]{1,0:T(8,128)(2,1)} %param.7) | copy-start | bytes 49156
  18.5 383.5 %all-reduce.2.cloned.1.call-start = ((), (), s32[]{:S(2)}) async-start(), calls=%async_computation.2 | async-start | bytes 4194304 | tf_op jit(solution)/shard_map/psum | solution.py:35
Sparse Core Ops, SparseCore 0:
  18.6 189.0 reduce-scatter.1
  211.7 190.2 all-reduce.1
where the time goes:
time: 443 us; the launch traced here: 440 us
  waiting for transfers between devices  377 us (85%)
  matrix products  18 us (4%)
  between operations  14.7 us (3%)
  local copies, waits for them, and re-layouts  13.1 us (3%)
  blocking collectives  9.01 us (2%)
  other arithmetic  8.19 us (2%)
    reduce_scatter x1, waiting for transfers between devices, on_device(): lax.psum_scatter(lax.dot_general(acts, grad_out, (((0,), (0,)), ((), ()))...  189 us
    psum x1, waiting for transfers between devices, on_device(): proj = lax.psum(partial_value, 'dp')  188 us
    unnamed x8, local copies, waits for them, and re-layouts  13.1 us
    dot_general x1, matrix products, on_device(): lax.dot_general(acts, grad_out, (((0,), (0,)), ((), ())), preferred_eleme...  9.69 us
    psum x1, blocking collectives, on_device(): energy = lax.psum(jnp.sum(proj * proj), 'group')  9.01 us
  transfers between devices with their start and end apart: 2, of which 2 were waited for; matrix products, arithmetic and copies ran while one was open for 1% of the time, Pallas kernels for 0%

commit v1 on v0

v1 whole, which is shorter than its diff:
```python
import functools
import math

import jax
import jax.numpy as jnp
from jax import lax
from jax.experimental import pallas as pl
from jax.experimental.pallas import tpu as pltpu
from jax.sharding import PartitionSpec as P

beta_one = 0.9
beta_two = 0.95
bias_one = 1.0 - 0.9**10
bias_two = 1.0 - 0.95**10
galore_scale = 0.25

MESH = pl.DeviceIdType.MESH
NZ, NY, NX = 8, 4, 4
SPAN = 250.0
HALF = 125.0
LN2 = math.log(2.0)
NEAR = (0, 1, 7, 2, 6, 3, 5, 4)
FAR = (4, 3, 5, 2, 6, 1, 7, 0)
f32 = jnp.float32
bf16 = jnp.bfloat16


def tiles_of(block):
    return [block[16 * r : 16 * r + 16, 128 * l : 128 * l + 128] for r in range(2) for l in range(2)]


def encode(tiles, packet):
    top = functools.reduce(jnp.maximum, [jnp.abs(t) for t in tiles])
    top = jnp.max(top, axis=0, keepdims=True)
    scale = (jnp.maximum(top, 1e-30) * 1.01).astype(bf16)
    packet[4] = jnp.broadcast_to(scale, (16, 128))
    rate = SPAN / scale.astype(f32)
    for i, t in enumerate(tiles):
        size = jnp.exp2(jnp.abs(t) * rate - HALF)
        packet[i] = jnp.where(t < 0, -size, size).astype(bf16)


def decode(packet):
    rate = packet[4].astype(f32) * (1.0 / (SPAN * LN2))
    out = []
    for i in range(4):
        code = packet[i].astype(f32)
        size = (jnp.log(jnp.abs(code)) + HALF * LN2) * rate
        out.append(jnp.where(code < 0, -size, size))
    return out


def reduce_kernel(
    acts, grad, p_ref, proj_out, energy_out,
    a_all, g_all, p_all, along, lhs, part, y_send, y_recv, z_send, z_recv, gathered, energies,
    load_sem, pair_send, pair_recv, pz_send, pz_recv, py_send, py_recv,
    ry_send, ry_recv, rz_send, rz_recv, az_send, az_recv, ay_send, ay_recv, ac_send, ac_recv, e_send, e_recv,
):
    dp = lax.axis_index("dp")
    x = lax.axis_index("group")
    c = lax.rem(dp, 2)
    y = lax.rem(lax.div(dp, 2), NY)
    z = lax.div(dp, 2 * NY)

    def at(zz, yy, cc, xx):
        return ((zz * NY + yy) * 2 + cc, xx)

    def zoff(d):
        return lax.rem(z + d, NZ)

    def yoff(d):
        return lax.rem(y + d, NY)

    def remote(src, dst, send, recv, device):
        return pltpu.make_async_remote_copy(
            src_ref=src, dst_ref=dst, send_sem=send, recv_sem=recv, device_id=device, device_id_type=MESH
        )

    me = at(z, y, c, x)
    sibling = at(z, y, 1 - c, x)
    loads = [
        pltpu.make_async_copy(acts, a_all.at[pl.ds(0, 512)], load_sem.at[0]),
        pltpu.make_async_copy(grad, g_all.at[pl.ds(0, 512)], load_sem.at[1]),
    ]
    for copy in loads:
        copy.start()

    barrier = pltpu.get_barrier_semaphore()
    peers = [at(zoff(d), y, cc, x) for d in range(1, NZ) for cc in range(2)]
    peers += [at(z, yoff(d), c, x) for d in range(1, NY)] + [sibling]
    peers += [at(z, y, c, lax.rem(x + d, NX)) for d in range(1, NX)]
    for peer in peers:
        pl.semaphore_signal(barrier, inc=1, device_id=peer, device_id_type=MESH)
    pl.semaphore_wait(barrier, len(peers))

    mine = pl.ds(pl.multiple_of((z * NY + y) * 64 + c * 32, 32), 32)
    for d in NEAR[::-1]:
        for cc in range(2):
            src = p_ref.at[:, pl.ds(cc * 128, 128)]
            if d:
                remote(src, p_all.at[mine], pz_send, pz_recv.at[d], at(zoff(d), y, cc, x)).start()
    for cc in range(2):

        @pl.when(c != cc)
        def _():
            remote(p_ref.at[:, pl.ds(cc * 128, 128)], p_all.at[mine], pz_send, pz_recv.at[0], sibling).start()

        @pl.when(c == cc)
        def _():
            p_all[mine, :] = p_ref[:, cc * 128 : cc * 128 + 128]

    pair = [
        remote(acts, a_all.at[pl.ds(512, 512)], pair_send.at[0], pair_recv.at[0], sibling),
        remote(grad, g_all.at[pl.ds(512, 512)], pair_send.at[1], pair_recv.at[1], sibling),
    ]
    for copy in pair:
        copy.start()

    def p_rows(zz, yy, n=64):
        return pl.ds(pl.multiple_of((zz * NY + yy) * 64, 64), n)

    def p_forward(d):
        zz = zoff(NZ - d)
        if d:
            remote(p_all.at[p_rows(zz, y)], p_all.at[p_rows(zz, y)], pz_send, pz_recv.at[d], me).wait_recv()
        else:
            remote(p_all.at[pl.ds(0, 32)], p_all.at[pl.ds(0, 32)], pz_send, pz_recv.at[0], me).wait_recv()
        for dy in range(1, NY):
            remote(
                p_all.at[p_rows(zz, y)], p_all.at[p_rows(zz, y)], py_send, py_recv.at[d], at(z, yoff(dy), c, x)
            ).start()

    def p_use(d, first):
        zz = zoff(NZ - d)
        three = p_all.at[pl.ds(0, 192)]
        remote(three, three, py_send, py_recv.at[d], me).wait_recv()
        if first:
            loads[0].wait()
            pair[0].wait_recv()
        cols = pl.ds(pl.multiple_of(zz * 256, 256), 256)
        term = jnp.dot(a_all[:, cols], p_all[p_rows(zz, 0, 256), :], preferred_element_type=f32)
        if first:
            along[...] = term
        else:
            along[...] += term

    lag = 3
    for k in range(NZ + lag):
        if k < NZ:
            p_forward(NEAR[k])
        if k >= lag:
            p_use(NEAR[k - lag], k == lag)

    turned = along[...].T
    high = turned.astype(bf16)
    lhs[pl.ds(0, 128), :] = high
    lhs[pl.ds(128, 128), :] = (turned - high.astype(f32)).astype(bf16)
    loads[1].wait()
    pair[1].wait_recv()

    for k, d in enumerate(FAR):
        cols = pl.ds(pl.multiple_of(zoff(d) * 256, 256), 256)
        both = jnp.dot(lhs[...], g_all[:, cols], preferred_element_type=f32)
        part[k] = both[:128] + both[128:]
        for dy in range(1, NY):
            yy = yoff(dy)
            encode(tiles_of(part[k, pl.ds(pl.multiple_of(yy * 32, 32), 32), :]), y_send.at[k, dy - 1])
            remote(y_send.at[k, dy - 1], y_recv.at[k, dy - 1], ry_send, ry_recv.at[k], at(z, yy, c, x)).start()

    all_p = p_all.at[pl.ds(0, 480)]
    remote(all_p, all_p, pz_send, pz_recv.at[0], me).wait_send()
    all_p = p_all.at[pl.ds(0, 1536)]
    remote(all_p, all_p, py_send, py_recv.at[0], me).wait_send()
    for copy in pair:
        copy.wait_send()

    own = pl.ds(pl.multiple_of(y * 32, 32), 32)
    total = None
    for k, d in enumerate(FAR):
        remote(y_recv.at[k], y_recv.at[k], ry_send, ry_recv.at[k], me).wait_recv()
        tiles = tiles_of(part[k, own, :])
        for i in range(NY - 1):
            tiles = [a + b for a, b in zip(tiles, decode(y_recv.at[k, i]))]
        if d:
            encode(tiles, z_send.at[d - 1])
            remote(z_send.at[d - 1], z_recv.at[d - 1], rz_send, rz_recv.at[d], at(zoff(d), y, c, x)).start()
        else:
            total = tiles
    for d in NEAR[1:]:
        remote(z_recv.at[d - 1], z_recv.at[d - 1], rz_send, rz_recv.at[d], me).wait_recv()
        total = [a + b for a, b in zip(total, decode(z_recv.at[d - 1]))]

    encode(total, gathered.at[c, z, y])
    for d in NEAR[:0:-1]:
        remote(
            gathered.at[c, z, y], gathered.at[c, z, y], az_send, az_recv.at[d], at(zoff(d), y, c, x)
        ).start()

    def out_forward(d):
        zz = zoff(NZ - d)
        block = gathered.at[c, zz, y]
        if d:
            remote(block, block, az_send, az_recv.at[d], me).wait_recv()
        for dy in range(1, NY):
            remote(block, block, ay_send, ay_recv.at[d], at(z, yoff(dy), c, x)).start()

    def out_share(d):
        zz = zoff(NZ - d)
        three = gathered.at[c, zz, pl.ds(0, 3)]
        remote(three, three, ay_send, ay_recv.at[d], me).wait_recv()
        remote(gathered.at[c, zz], gathered.at[c, zz], ac_send, ac_recv.at[d], sibling).start()

    for k in range(NZ + lag):
        if k < NZ:
            out_forward(NEAR[k])
        if k >= lag:
            out_share(NEAR[k - lag])

    energies[0] = jnp.zeros((8, 128), f32)

    def unpack(cc, zz):
        energy = energies[0]
        for yy in range(NY):
            tiles = decode(gathered.at[cc, zz, yy])
            for i, t in enumerate(tiles):
                rows = pl.ds(pl.multiple_of(cc * 128 + yy * 32 + (i // 2) * 16, 16), 16)
                cols = pl.ds(pl.multiple_of(zz * 256 + (i % 2) * 128, 128), 128)
                proj_out[rows, cols] = t
                square = t * t
                energy = energy + square[:8] + square[8:]
        energies[0] = energy

    def unpack_own(zz, carry):
        unpack(c, zz)
        return carry

    lax.fori_loop(0, NZ, unpack_own, 0)
    for d in NEAR:
        zz = zoff(NZ - d)
        theirs = gathered.at[1 - c, zz]
        remote(theirs, theirs, ac_send, ac_recv.at[d], me).wait_recv()
        unpack(1 - c, zz)

    for d in range(1, NX):
        remote(
            energies.at[0], energies.at[d], e_send.at[d], e_recv.at[d], at(z, y, c, lax.rem(x + d, NX))
        ).start()
    all_y = y_send
    remote(all_y, all_y, ry_send, ry_recv.at[0], me).wait_send()
    remote(z_send, z_send, rz_send, rz_recv.at[1], me).wait_send()
    seven = z_send
    remote(seven, seven, az_send, az_recv.at[1], me).wait_send()
    many = gathered.at[0, pl.ds(0, 6)]
    remote(many, many, ay_send, ay_recv.at[0], me).wait_send()
    many = gathered.at[0]
    remote(many, many, ac_send, ac_recv.at[0], me).wait_send()
    energy = energies[0]
    for d in range(1, NX):
        remote(energies.at[0], energies.at[d], e_send.at[d], e_recv.at[d], me).wait()
        energy = energy + energies[d]
    energy_out[...] = energy


def reduced(acts, grad_out, projector):
    sem = pltpu.SemaphoreType.DMA
    any_space = pl.BlockSpec(memory_space=pl.ANY)
    vmem = pl.BlockSpec(memory_space=pltpu.VMEM)
    return pl.pallas_call(
        reduce_kernel,
        name="projected_gradient",
        out_shape=(jax.ShapeDtypeStruct((256, 2048), f32), jax.ShapeDtypeStruct((8, 128), f32)),
        in_specs=[any_space, any_space, vmem],
        out_specs=(vmem, vmem),
        scratch_shapes=[
            pltpu.VMEM((1024, 2048), bf16),
            pltpu.VMEM((1024, 2048), bf16),
            pltpu.VMEM((2048, 128), bf16),
            pltpu.VMEM((1024, 128), f32),
            pltpu.VMEM((256, 1024), bf16),
            pltpu.VMEM((NZ, 128, 256), f32),
            pltpu.VMEM((NZ, NY - 1, 5, 16, 128), bf16),
            pltpu.VMEM((NZ, NY - 1, 5, 16, 128), bf16),
            pltpu.VMEM((NZ - 1, 5, 16, 128), bf16),
            pltpu.VMEM((NZ - 1, 5, 16, 128), bf16),
            pltpu.VMEM((2, NZ, NY, 5, 16, 128), bf16),
            pltpu.VMEM((NX, 8, 128), f32),
            sem((2,)), sem((2,)), sem((2,)),
            sem, sem((NZ,)), sem, sem((NZ,)),
            sem, sem((NZ,)), sem, sem((NZ,)),
            sem, sem((NZ,)), sem, sem((NZ,)), sem, sem((NZ,)),
            sem((NX,)), sem((NX,)),
        ],
        compiler_params=pltpu.CompilerParams(
            collective_id=0, has_side_effects=True, vmem_limit_bytes=32 * 1024 * 1024
        ),
        cost_estimate=pl.CostEstimate(flops=1 << 31, bytes_accessed=6 << 20, transcendentals=1 << 20),
    )(acts, grad_out, projector)


def update_kernel(entries, proj, energy, projector, first_old, second_old, update, first_new, second_new):
    mean = jnp.sum(energy[...]) / entries
    clip = jnp.minimum(1.0, 1.0 / jnp.sqrt(jnp.full((1, 128), mean + 1e-06, f32)))
    clip = jnp.concatenate([clip, clip], axis=1)
    clipped = clip * proj[...]
    first = beta_one * first_old[...] + (1.0 - beta_one) * clipped
    second = beta_two * second_old[...] + (1.0 - beta_two) * clipped * clipped
    first_new[...] = first
    second_new[...] = second
    direction = first * (1.0 / bias_one) / (jnp.sqrt(second * (1.0 / bias_two)) + 1e-08)
    high = direction.astype(bf16)
    low = (direction - high.astype(f32)).astype(bf16)
    rows = projector[...]
    moved = jnp.dot(rows, high, preferred_element_type=f32) + jnp.dot(rows, low, preferred_element_type=f32)
    update[...] = galore_scale * moved


def updated(proj, energy, projector, moment_one, moment_two, entries):
    wide = pl.BlockSpec((256, 256), lambda i: (0, i))
    return pl.pallas_call(
        functools.partial(update_kernel, entries),
        name="adam_update",
        grid=(8,),
        out_shape=(
            jax.ShapeDtypeStruct((32, 2048), f32),
            jax.ShapeDtypeStruct((256, 2048), f32),
            jax.ShapeDtypeStruct((256, 2048), f32),
        ),
        in_specs=[
            wide,
            pl.BlockSpec((8, 128), lambda i: (0, 0)),
            pl.BlockSpec((32, 256), lambda i: (0, 0)),
            wide,
            wide,
        ],
        out_specs=(pl.BlockSpec((32, 256), lambda i: (0, i)), wide, wide),
        cost_estimate=pl.CostEstimate(flops=1 << 26, bytes_accessed=10 << 20, transcendentals=1 << 20),
    )(proj, energy, projector, moment_one, moment_two)


def on_device(acts, grad_out, projector, moment_one, moment_two):
    entries = float(projector.shape[1] * grad_out.shape[1] * NX)
    proj, energy = reduced(acts, grad_out, projector)
    return updated(proj, energy, projector, moment_one, moment_two, entries)


def solution(mesh):
    placed = (P("dp", None), P("dp", "group"), P("dp", None), P(None, "group"), P(None, "group"))
    return jax.shard_map(
        on_device,
        mesh=mesh,
        in_specs=placed,
        out_specs=(P("dp", "group"), P(None, "group"), P(None, "group")),
        check_vma=False,
    )
```

time: 443 us -> 70.5 us (0.16)
  waiting for transfers between devices: 377 us -> 0 us
  Pallas kernels: 0 us -> 63.6 us
  matrix products: 18 us -> 0 us
  between operations: 14.7 us -> 0.66 us
  blocking collectives: 9.01 us -> 0 us
  other arithmetic: 8.19 us -> 0 us
  local copies, waits for them, and re-layouts: 13.1 us -> 5.82 us
    reduce_scatter x1 -> x0, waiting for transfers between devices: 189 us -> none  [on_device(): lax.psum_scatter(lax.dot_general(acts, grad_out, (((0,), (0,)), ((), ()))...]
    psum x1 -> x0, waiting for transfers between devices: 188 us -> none  [on_device(): proj = lax.psum(partial_value, 'dp')]
    pallas_call x0 -> x2, Pallas kernels: none -> 63.6 us  [the longest x1 55.7 us: reduced(): pl.pallas_call(reduce_kernel, name='projected_gradient', out_shape=(jax.S...]
    dot_general x3 -> x0, matrix products: 18 us -> none  [the longest x1 9.69 us: on_device(): lax.dot_general(acts, grad_out, (((0,), (0,)), ((), ())), preferred_eleme...]
    psum x1 -> x0, blocking collectives: 9.01 us -> none  [on_device(): energy = lax.psum(jnp.sum(proj * proj), 'group')]
    unnamed x8 -> x10, local copies, waits for them, and re-layouts: 13.1 us -> 5.82 us
    add x1 -> x0, other arithmetic: 5.46 us -> none  [adam_moments(): first = beta_one * first_old + (1.0 - beta_one) * clipped]
  transfers between devices with their start and end apart: 2 -> 0, of which waited for: 2 -> 0; matrix products, arithmetic and copies ran while one was open for 1% -> 0% of each run, Pallas kernels for 0% -> 0%
where the time goes in v1:
time: 70.5 us; the launch traced here: 70.1 us
  Pallas kernels  63.6 us (90%)
  local copies, waits for them, and re-layouts  5.82 us (8%)
    pallas_call x1, Pallas kernels, reduced(): pl.pallas_call(reduce_kernel, name='projected_gradient', out_shape=(jax.S...  55.7 us
    pallas_call x1, Pallas kernels, updated(): pl.pallas_call(functools.partial(update_kernel, entries), name='adam_upda...  7.91 us
    unnamed x10, local copies, waits for them, and re-layouts  5.82 us

profile of v1, /device:TPU:1, one launch (start us, length us, event | category | flops | bytes accessed | tf_op | source)
XLA Modules:
  0.0 70.1 jit_solution(7737748346717559577)
XLA Ops:
  0.6 0.0 copy-start.1
  0.6 0.7 %copy-done.1 = bf16[32,256]{1,0:T(8,128)(2,1)S(1)} copy-done((bf16[32,256]{1,0:T(8,128)(2,1)S(1)}, bf16[32,256]{1,0:T(8,128)(2,1)}, u32[]{:S(2)}) %copy-start.1) | copy-done | bytes 16408
  1.4 0.0 copy-start.3
  1.4 1.6 %copy-done.3 = bf16[512,2048]{1,0:T(8,128)(2,1)S(1)} copy-done((bf16[512,2048]{1,0:T(8,128)(2,1)S(1)}, bf16[512,2048]{1,0:T(8,128)(2,1)}, u32[]{:S(2)}) %copy-start.3) | copy-done | bytes 2097176
  2.9 0.0 copy-start.4
  2.9 1.6 %copy-done.4 = bf16[512,2048]{1,0:T(8,128)(2,1)S(1)} copy-done((bf16[512,2048]{1,0:T(8,128)(2,1)S(1)}, bf16[512,2048]{1,0:T(8,128)(2,1)}, u32[]{:S(2)}) %copy-start.4) | copy-done | bytes 2097176
  4.5 55.7 %projected_gradient.1 = (f32[256,2048]{1,0:T(8,128)S(1)}, f32[8,128]{1,0:T(8,128)S(1)}) custom-call(bf16[512,2048]{1,0:T(8,128)(2,1)S(1)} %copy-done.3, bf16[512,2048]{1,0:T(8,128)(2,1)S(1)} %copy-done.4, bf16[32,256]{1,0:T(8,128)(2,1)S(1)} %copy-done.1), custom_call_target="tpu_custom_call" | custom-call | flops 2147483648 | bytes 6291456 | tf_op jit(solution)/shard_map/projected_gradient/pallas_call | solution.py:268
  60.3 0.0 copy-start
  60.3 1.3 %copy-done = f32[256,2048]{1,0:T(8,128)} copy-done((f32[256,2048]{1,0:T(8,128)}, f32[256,2048]{1,0:T(8,128)S(1)}, u32[]{:S(2)}) %copy-start) | copy-done | bytes 2097176
  61.6 0.0 copy-start.2
  61.6 0.6 copy-done.2
  62.2 7.9 %adam_update.1 = (f32[32,2048]{1,0:T(8,128)}, f32[256,2048]{1,0:T(8,128)}, f32[256,2048]{1,0:T(8,128)}) custom-call(f32[256,2048]{1,0:T(8,128)} %copy-done, f32[8,128]{1,0:T(8,128)} %copy-done.2, bf16[32,256]{1,0:T(8,128)(2,1)} %projector.1, f32[256,2048]{1,0:T(8,128)} %first_old.1, f32[256,2048]{1,0:T(8,128)} %second_old.1), custom_call_target="tpu_custom_call" | custom-call | flops 67108864 | bytes 10485760 | tf_op jit(solution)/shard_map/adam_update/pallas_call | solution.py:319
Async XLA Ops:
  0.6 0.7 %copy-start.1 = (bf16[32,256]{1,0:T(8,128)(2,1)S(1)}, bf16[32,256]{1,0:T(8,128)(2,1)}, u32[]{:S(2)}) copy-start(bf16[32,256]{1,0:T(8,128)(2,1)} %projector.1) | copy-start | bytes 49156
  1.4 1.6 %copy-start.3 = (bf16[512,2048]{1,0:T(8,128)(2,1)S(1)}, bf16[512,2048]{1,0:T(8,128)(2,1)}, u32[]{:S(2)}) copy-start(bf16[512,2048]{1,0:T(8,128)(2,1)} %acts.1) | copy-start | bytes 6291460
  2.9 1.6 %copy-start.4 = (bf16[512,2048]{1,0:T(8,128)(2,1)S(1)}, bf16[512,2048]{1,0:T(8,128)(2,1)}, u32[]{:S(2)}) copy-start(bf16[512,2048]{1,0:T(8,128)(2,1)} %grad.1) | copy-start | bytes 6291460
  60.3 1.3 %copy-start = (f32[256,2048]{1,0:T(8,128)}, f32[256,2048]{1,0:T(8,128)S(1)}, u32[]{:S(2)}) copy-start(f32[256,2048]{1,0:T(8,128)S(1)} %get-tuple-element.5.proj) | copy-start | bytes 6291460
  61.6 0.6 copy-start.2

commit v2 on v1

v2 whole, which is shorter than its diff:
```python
import functools
import math

import jax
import jax.numpy as jnp
from jax import lax
from jax.experimental import pallas as pl
from jax.experimental.pallas import tpu as pltpu
from jax.sharding import PartitionSpec as P

beta_one = 0.9
beta_two = 0.95
bias_one = 1.0 - 0.9**10
bias_two = 1.0 - 0.95**10
galore_scale = 0.25

MESH = pl.DeviceIdType.MESH
NZ, NY, NX = 8, 4, 4
SPAN = 250.0
HALF = 125.0
LN2 = math.log(2.0)
NEAR = (0, 1, 7, 2, 6, 3, 5, 4)
FAR = (4, 3, 5, 2, 6, 1, 7, 0)
f32 = jnp.float32
bf16 = jnp.bfloat16


def tiles_of(block):
    return [block[16 * r : 16 * r + 16, 128 * l : 128 * l + 128] for r in range(2) for l in range(2)]


def scale_of(tiles):
    top = functools.reduce(jnp.maximum, [jnp.abs(t) for t in tiles])
    top = jnp.max(top, axis=0, keepdims=True)
    return (jnp.maximum(top, 1e-30) * 1.01).astype(bf16).astype(f32)


def encode(tiles, scale):
    rate = SPAN / scale
    out = []
    for t in tiles:
        size = jnp.exp2(jnp.abs(t) * rate - HALF)
        out.append(jnp.where(t < 0, -size, size).astype(bf16))
    return out


def decode(codes, scale):
    rate = scale * (1.0 / (SPAN * LN2))
    out = []
    for code in codes:
        code = code.astype(f32)
        size = (jnp.log(jnp.abs(code)) + HALF * LN2) * rate
        out.append(jnp.where(code < 0, -size, size))
    return out


def reduce_kernel(
    entries, acts, grad, p_hbm, proj_out, clip_out,
    p_ref, a_all, g_all, p_all, along, lhs, part, y_send, y_recv, z_send, z_recv, gathered, sums,
    load_sem, pair_send, pair_recv, pz_send, pz_recv, py_send, py_recv,
    ry_send, ry_recv, rz_send, rz_recv, az_send, az_recv, ay_send, ay_recv, ac_send, ac_recv,
    ex_send, ex_recv, ey_send, ey_recv,
):
    dp = lax.axis_index("dp")
    x = lax.axis_index("group")
    c = lax.rem(dp, 2)
    y = lax.rem(lax.div(dp, 2), NY)
    z = lax.div(dp, 2 * NY)

    def at(zz, yy, cc, xx):
        return ((zz * NY + yy) * 2 + cc, xx)

    def zoff(d):
        return lax.rem(z + d, NZ)

    def yoff(d):
        return lax.rem(y + d, NY)

    def xoff(d):
        return lax.rem(x + d, NX)

    def remote(src, dst, send, recv, device):
        return pltpu.make_async_remote_copy(
            src_ref=src, dst_ref=dst, send_sem=send, recv_sem=recv, device_id=device, device_id_type=MESH
        )

    me = at(z, y, c, x)
    sibling = at(z, y, 1 - c, x)

    def arrived(ref, recv):
        remote(ref, ref, pz_send, recv, me).wait_recv()

    def sent(ref, send):
        remote(ref, ref, send, pz_recv.at[0], me).wait_send()

    loads = [
        pltpu.make_async_copy(p_hbm, p_ref, load_sem.at[2]),
        pltpu.make_async_copy(acts, a_all.at[pl.ds(0, 512)], load_sem.at[0]),
        pltpu.make_async_copy(grad, g_all.at[pl.ds(0, 512)], load_sem.at[1]),
    ]
    for copy in loads:
        copy.start()

    barrier = pltpu.get_barrier_semaphore()
    peers = [at(zoff(d), y, cc, x) for d in NEAR[:0:-1] for cc in range(2)]
    peers += [at(z, yoff(d), cc, x) for d in range(1, NY) for cc in range(2)] + [sibling]
    peers += [at(z, y, c, xoff(d)) for d in range(1, NX)]
    for peer in peers:
        pl.semaphore_signal(barrier, inc=1, device_id=peer, device_id_type=MESH)
    loads[0].wait()
    pl.semaphore_wait(barrier, len(peers))

    mine = pl.ds(pl.multiple_of((z * NY + y) * 64 + c * 32, 32), 32)
    for cc in range(2):

        @pl.when(c != cc)
        def _():
            remote(p_ref.at[:, pl.ds(cc * 128, 128)], p_all.at[mine], pz_send, pz_recv.at[0], sibling).start()

        @pl.when(c == cc)
        def _():
            p_all[mine, :] = p_ref[:, cc * 128 : cc * 128 + 128]

    for d in NEAR[:0:-1]:
        for cc in range(2):
            src = p_ref.at[:, pl.ds(cc * 128, 128)]
            remote(src, p_all.at[mine], pz_send, pz_recv.at[d], at(zoff(d), y, cc, x)).start()

    pair = [
        remote(acts, a_all.at[pl.ds(512, 512)], pair_send.at[0], pair_recv.at[0], sibling),
        remote(grad, g_all.at[pl.ds(512, 512)], pair_send.at[1], pair_recv.at[1], sibling),
    ]
    for copy in pair:
        copy.start()

    def p_rows(zz, yy, n=64):
        return pl.ds(pl.multiple_of((zz * NY + yy) * 64, 64), n)

    def p_forward(d):
        chunk = p_all.at[p_rows(zoff(NZ - d), y)]
        arrived(chunk if d else p_all.at[pl.ds(0, 32)], pz_recv.at[d])
        for dy in (2, 1, 3):
            remote(chunk, chunk, py_send, py_recv.at[d], at(z, yoff(dy), c, x)).start()

    def p_use(d, first):
        zz = zoff(NZ - d)
        arrived(p_all.at[pl.ds(0, 192)], py_recv.at[d])
        if first:
            loads[1].wait()
            pair[0].wait_recv()
        cols = pl.ds(pl.multiple_of(zz * 256, 256), 256)
        term = jnp.dot(a_all[:, cols], p_all[p_rows(zz, 0, 256), :], preferred_element_type=f32)
        if first:
            along[...] = term
        else:
            along[...] += term

    lag = 4
    for k in range(NZ + lag):
        if k < NZ:
            p_forward(NEAR[k])
        if k >= lag:
            p_use(NEAR[k - lag], k == lag)

    turned = along[...].T
    high = turned.astype(bf16)
    lhs[pl.ds(0, 128), :] = high
    lhs[pl.ds(128, 128), :] = (turned - high.astype(f32)).astype(bf16)
    loads[2].wait()
    pair[1].wait_recv()

    row = lax.broadcasted_iota(jnp.int32, (16, 128), 0)
    for k, d in enumerate(FAR):
        cols = pl.ds(pl.multiple_of(zoff(d) * 256, 256), 256)
        both = jnp.dot(lhs[...], g_all[:, cols], preferred_element_type=f32)
        part[k] = both[:128] + both[128:]
        if k % 2 == 0:
            continue
        for dy in (2, 1, 3):
            yy = yoff(dy)
            message = y_send.at[k // 2, dy - 1]
            scales = []
            for j in range(2):
                tiles = tiles_of(part[k - 1 + j, pl.ds(pl.multiple_of(yy * 32, 32), 32), :])
                scales.append(scale_of(tiles))
                for i, code in enumerate(encode(tiles, scales[j])):
                    message[4 * j + i] = code
            message[8] = jnp.where(row < 8, scales[0], scales[1]).astype(bf16)
            remote(
                message, y_recv.at[k // 2, dy - 1], ry_send, ry_recv.at[k // 2], at(z, yy, c, x)
            ).start()

    sent(p_all.at[pl.ds(0, 480)], pz_send)
    sent(p_all.at[pl.ds(0, 1536)], py_send)
    for copy in pair:
        copy.wait_send()

    own = pl.ds(pl.multiple_of(y * 32, 32), 32)
    for k, d in enumerate(FAR):
        if k % 2 == 0:
            arrived(y_recv.at[k // 2], ry_recv.at[k // 2])
        total = tiles_of(part[k, own, :])
        for i in range(NY - 1):
            message = y_recv.at[k // 2, i]
            scale = message[8][8 * (k % 2) : 8 * (k % 2) + 1].astype(f32)
            codes = [message[4 * (k % 2) + j] for j in range(4)]
            total = [a + b for a, b in zip(total, decode(codes, scale))]
        if d:
            packet = z_send.at[d - 1]
            scale = scale_of(total)
            for i, code in enumerate(encode(total, scale)):
                packet[i] = code
            packet[4] = jnp.broadcast_to(scale, (16, 128)).astype(bf16)
            remote(packet, z_recv.at[d - 1], rz_send, rz_recv.at[d], at(zoff(d), y, c, x)).start()
    sent(y_send, ry_send)
    for d in NEAR[1:]:
        packet = z_recv.at[d - 1]
        arrived(packet, rz_recv.at[d])
        codes = [packet[j] for j in range(4)]
        total = [a + b for a, b in zip(total, decode(codes, packet[4][:1].astype(f32)))]

    packet = gathered.at[c, z, y]
    scale = scale_of(total)
    energy = jnp.sum(functools.reduce(jnp.add, [t * t for t in total]), axis=0, keepdims=True)
    e_high = energy.astype(bf16).astype(f32)
    e_mid = (energy - e_high).astype(bf16).astype(f32)
    e_low = energy - e_high - e_mid
    for i, code in enumerate(encode(total, scale)):
        packet[i] = code
    last = jnp.where(row < 8, scale, 0.0)
    for i, part_of in enumerate((e_high, e_mid, e_low)):
        last = jnp.where(row == 8 + i, part_of, last)
    packet[4] = last.astype(bf16)
    for d in NEAR[:0:-1]:
        remote(packet, packet, az_send, az_recv.at[d], at(zoff(d), y, c, x)).start()

    def out_forward(d):
        block = gathered.at[c, zoff(NZ - d), y]
        if d:
            arrived(block, az_recv.at[d])
        for dy in (2, 1, 3):
            remote(block, block, ay_send, ay_recv.at[d], at(z, yoff(dy), c, x)).start()

    def out_share(d):
        zz = zoff(NZ - d)
        arrived(gathered.at[c, zz, pl.ds(0, 3)], ay_recv.at[d])
        remote(gathered.at[c, zz], gathered.at[c, zz], ac_send, ac_recv.at[d], sibling).start()

    for k in range(NZ):
        out_forward(NEAR[k])
    sent(z_send, rz_send)

    tile = functools.reduce(jnp.add, [gathered[c, zz, y, 4].astype(f32) for zz in range(NZ)])
    sums[0] = jnp.where(lax.broadcasted_iota(jnp.int32, (8, 128), 0) < 3, tile[8:], 0.0)
    for d in (2, 1, 3):
        remote(sums.at[0], sums.at[d], ex_send, ex_recv, at(z, y, c, xoff(d))).start()
    for k in range(NZ // 2):
        out_share(NEAR[k])
    arrived(sums.at[pl.ds(0, 3)], ex_recv)
    sums[4] = sums[0] + sums[1] + sums[2] + sums[3]
    slot = 5
    for dy in (2, 1, 3, 0):
        for dc in (1, 0):
            if dy or dc:
                cc = lax.rem(c + dc, 2)
                remote(sums.at[4], sums.at[slot], ey_send, ey_recv, at(z, yoff(dy), cc, x)).start()
                slot += 1
    for k in range(NZ // 2, NZ):
        out_share(NEAR[k])

    def unpack(cc, zz):
        for yy in range(NY):
            source = gathered.at[cc, zz, yy]
            codes = [source[j] for j in range(4)]
            for i, t in enumerate(decode(codes, source[4][:1].astype(f32))):
                rows = pl.ds(pl.multiple_of(cc * 128 + yy * 32 + (i // 2) * 16, 16), 16)
                cols = pl.ds(pl.multiple_of(zz * 256 + (i % 2) * 128, 128), 128)
                proj_out[rows, cols] = t

    def unpack_own(zz, carry):
        unpack(c, zz)
        return carry

    lax.fori_loop(0, NZ, unpack_own, 0)
    arrived(sums.at[pl.ds(0, 7)], ey_recv)
    energy = functools.reduce(jnp.add, [sums[i] for i in range(4, 12)])
    mean = jnp.full((8, 128), jnp.sum(energy) / entries + 1e-06, f32)
    clip_out[...] = jnp.minimum(1.0, 1.0 / jnp.sqrt(mean))
    for d in NEAR:
        zz = zoff(NZ - d)
        arrived(gathered.at[1 - c, zz], ac_recv.at[d])
        unpack(1 - c, zz)

    sent(z_send, az_send)
    sent(gathered.at[0, pl.ds(0, 6)], ay_send)
    sent(gathered.at[0], ac_send)
    sent(sums.at[pl.ds(0, 3)], ex_send)
    sent(sums.at[pl.ds(0, 7)], ey_send)


def reduced(acts, grad_out, projector, entries):
    sem = pltpu.SemaphoreType.DMA
    hbm = pl.BlockSpec(memory_space=pltpu.HBM)
    vmem = pl.BlockSpec(memory_space=pltpu.VMEM)
    return pl.pallas_call(
        functools.partial(reduce_kernel, entries),
        name="projected_gradient",
        out_shape=(jax.ShapeDtypeStruct((256, 2048), f32), jax.ShapeDtypeStruct((8, 128), f32)),
        in_specs=[hbm, hbm, hbm],
        out_specs=(vmem, vmem),
        scratch_shapes=[
            pltpu.VMEM((32, 256), bf16),
            pltpu.VMEM((1024, 2048), bf16),
            pltpu.VMEM((1024, 2048), bf16),
            pltpu.VMEM((2048, 128), bf16),
            pltpu.VMEM((1024, 128), f32),
            pltpu.VMEM((256, 1024), bf16),
            pltpu.VMEM((NZ, 128, 256), f32),
            pltpu.VMEM((NZ // 2, NY - 1, 9, 16, 128), bf16),
            pltpu.VMEM((NZ // 2, NY - 1, 9, 16, 128), bf16),
            pltpu.VMEM((NZ - 1, 5, 16, 128), bf16),
            pltpu.VMEM((NZ - 1, 5, 16, 128), bf16),
            pltpu.VMEM((2, NZ, NY, 5, 16, 128), bf16),
            pltpu.VMEM((12, 8, 128), f32),
            sem((3,)), sem((2,)), sem((2,)),
            sem, sem((NZ,)), sem, sem((NZ,)),
            sem, sem((NZ // 2,)), sem, sem((NZ,)),
            sem, sem((NZ,)), sem, sem((NZ,)), sem, sem((NZ,)),
            sem, sem, sem, sem,
        ],
        compiler_params=pltpu.CompilerParams(
            collective_id=0, has_side_effects=True, vmem_limit_bytes=20 * 1024 * 1024
        ),
        cost_estimate=pl.CostEstimate(flops=1 << 31, bytes_accessed=6 << 20, transcendentals=1 << 20),
    )(acts, grad_out, projector)


def update_kernel(
    proj, clip, projector, first_old, second_old, update, first_new, second_new, u_out, f_out, s_out, sem
):
    scale = clip[:1, :]
    scale = jnp.concatenate([scale, scale], axis=1)
    rows = projector[...]
    copies = []
    for i in range(8):
        cols = pl.ds(256 * i, 256)
        clipped = scale * proj[:, cols]
        first = beta_one * first_old[:, cols] + (1.0 - beta_one) * clipped
        second = beta_two * second_old[:, cols] + (1.0 - beta_two) * clipped * clipped
        f_out[:, cols] = first
        s_out[:, cols] = second
        for j, (src, dst) in enumerate(((f_out, first_new), (s_out, second_new))):
            copies.append(pltpu.make_async_copy(src.at[:, cols], dst.at[:, cols], sem.at[i, j]))
            copies[-1].start()
        direction = first * (1.0 / bias_one) / (jnp.sqrt(second * (1.0 / bias_two)) + 1e-08)
        high = direction.astype(bf16)
        low = (direction - high.astype(f32)).astype(bf16)
        moved = jnp.dot(rows, high, preferred_element_type=f32) + jnp.dot(rows, low, preferred_element_type=f32)
        u_out[:, cols] = galore_scale * moved
        copies.append(pltpu.make_async_copy(u_out.at[:, cols], update.at[:, cols], sem.at[i, 2]))
        copies[-1].start()
    for copy in copies:
        copy.wait()


def updated(proj, clip, projector, moment_one, moment_two):
    hbm = pl.BlockSpec(memory_space=pltpu.HBM)
    vmem = pl.BlockSpec(memory_space=pltpu.VMEM)
    return pl.pallas_call(
        update_kernel,
        name="adam_update",
        out_shape=(
            jax.ShapeDtypeStruct((32, 2048), f32),
            jax.ShapeDtypeStruct((256, 2048), f32),
            jax.ShapeDtypeStruct((256, 2048), f32),
        ),
        in_specs=[vmem] * 5,
        out_specs=(hbm, hbm, hbm),
        scratch_shapes=[
            pltpu.VMEM((32, 2048), f32),
            pltpu.VMEM((256, 2048), f32),
            pltpu.VMEM((256, 2048), f32),
            pltpu.SemaphoreType.DMA((8, 3)),
        ],
        compiler_params=pltpu.CompilerParams(vmem_limit_bytes=16 * 1024 * 1024),
        cost_estimate=pl.CostEstimate(flops=1 << 26, bytes_accessed=10 << 20, transcendentals=1 << 20),
    )(proj, clip, projector, moment_one, moment_two)


def on_device(acts, grad_out, projector, moment_one, moment_two):
    entries = float(projector.shape[1] * grad_out.shape[1] * NX)
    acts, grad_out, rows = (pltpu.with_memory_space_constraint(a, pltpu.HBM) for a in (acts, grad_out, projector))
    proj, clip = reduced(acts, grad_out, rows, entries)
    return updated(proj, clip, projector, moment_one, moment_two)


def solution(mesh):
    placed = (P("dp", None), P("dp", "group"), P("dp", None), P(None, "group"), P(None, "group"))
    return jax.shard_map(
        on_device,
        mesh=mesh,
        in_specs=placed,
        out_specs=(P("dp", "group"), P(None, "group"), P(None, "group")),
        check_vma=False,
    )
```

time: 70.5 us -> 54.1 us (0.77)
  Pallas kernels: 63.6 us -> 53.3 us
  local copies, waits for them, and re-layouts: 5.82 us -> 0.01 us
    pallas_call x2, Pallas kernels: 63.6 us -> 53.3 us  [the longest x1 49.6 us: reduced(): pl.pallas_call(functools.partial(reduce_kernel, entries), name='projected...]
    unnamed x10 -> x6, local copies, waits for them, and re-layouts: 5.82 us -> 0.01 us
where the time goes in v2:
time: 54.1 us; the launch traced here: 54 us
  Pallas kernels  53.3 us (99%)
  between operations  0.69 us (1%)
    pallas_call x1, Pallas kernels, reduced(): pl.pallas_call(functools.partial(reduce_kernel, entries), name='projected...  49.6 us
    pallas_call x1, Pallas kernels, updated(): pl.pallas_call(update_kernel, name='adam_update', out_shape=(jax.ShapeDty...  3.76 us

profile of v2, /device:TPU:1, one launch (start us, length us, event | category | flops | bytes accessed | tf_op | source)
XLA Modules:
  0.0 54.0 jit_solution(15806677730709659913)
XLA Ops:
  0.6 0.0 copy-start.2
  0.6 0.0 copy-start.1
  0.7 0.0 copy-start
  0.7 49.6 %projected_gradient.1 = (f32[256,2048]{1,0:T(8,128)S(1)}, f32[8,128]{1,0:T(8,128)S(1)}) custom-call(bf16[512,2048]{1,0:T(8,128)(2,1)} %acts.1, bf16[512,2048]{1,0:T(8,128)(2,1)} %grad.1, bf16[32,256]{1,0:T(8,128)(2,1)} %projector.1), custom_call_target="tpu_custom_call" | custom-call | flops 2147483648 | bytes 6291456 | tf_op jit(solution)/shard_map/projected_gradient/pallas_call | solution.py:305
  50.2 0.0 copy-done.2
  50.3 0.0 copy-done.1
  50.3 0.0 copy-done
  50.3 3.8 %adam_update.1 = (f32[32,2048]{1,0:T(8,128)}, f32[256,2048]{1,0:T(8,128)}, f32[256,2048]{1,0:T(8,128)}) custom-call(f32[256,2048]{1,0:T(8,128)S(1)} %get-tuple-element.5.proj, f32[8,128]{1,0:T(8,128)S(1)} %get-tuple-element.6.clip, bf16[32,256]{1,0:T(8,128)(2,1)S(1)} %copy-done.2, f32[256,2048]{1,0:T(8,128)S(1)} %copy-done, f32[256,2048]{1,0:T(8,128)S(1)} %copy-done.1), custom_call_target="tpu_custom_call" | custom-call | flops 67108864 | bytes 10485760 | tf_op jit(solution)/shard_map/adam_update/pallas_call | solution.py:369
Async XLA Ops:
  0.6 49.6 %copy-start.2 = (bf16[32,256]{1,0:T(8,128)(2,1)S(1)}, bf16[32,256]{1,0:T(8,128)(2,1)}, u32[]{:S(2)}) copy-start(bf16[32,256]{1,0:T(8,128)(2,1)} %projector.1) | copy-start | bytes 49156
  0.6 49.6 %copy-start.1 = (f32[256,2048]{1,0:T(8,128)S(1)}, f32[256,2048]{1,0:T(8,128)}, u32[]{:S(2)}) copy-start(f32[256,2048]{1,0:T(8,128)} %second_old.1) | copy-start | bytes 6291460
  0.7 49.6 %copy-start = (f32[256,2048]{1,0:T(8,128)S(1)}, f32[256,2048]{1,0:T(8,128)}, u32[]{:S(2)}) copy-start(f32[256,2048]{1,0:T(8,128)} %first_old.1) | copy-start | bytes 6291460

commit v3 on v2

--- a/solution.py
+++ b/solution.py
@@ -56,10 +56,13 @@
 
 def reduce_kernel(
     entries, acts, grad, p_hbm, proj_out, clip_out,
-    p_ref, a_all, g_all, p_all, along, lhs, part, y_send, y_recv, z_send, z_recv, gathered, sums,
+    p_ref, a_all, g_all, p_all, along, lhs, part,
+    yb_send, yb_recv, za_send, za_recv, zb_send, zb_recv, ya_send, ya_recv,
+    column, three_all, fourth_all, scale_all, scale_wide, sums,
     load_sem, pair_send, pair_recv, pz_send, pz_recv, py_send, py_recv,
-    ry_send, ry_recv, rz_send, rz_recv, az_send, az_recv, ay_send, ay_recv, ac_send, ac_recv,
-    ex_send, ex_recv, ey_send, ey_recv,
+    yb_sent, yb_came, za_sent, za_came, zb_sent, zb_came, ya_sent, ya_came,
+    az_sent, az_came, ay_sent, ay_came, by_sent, by_came, bz_sent, bz_came,
+    sy_sent, sy_came, sc_sent, sc_came, ac_sent, ac_came, ex_send, ex_recv, ey_send, ey_recv,
 ):
     dp = lax.axis_index("dp")
     x = lax.axis_index("group")
@@ -170,24 +173,44 @@
     pair[1].wait_recv()
 
     row = lax.broadcasted_iota(jnp.int32, (16, 128), 0)
+
+    def block_rows(dy, rh, n):
+        return pl.ds(pl.multiple_of(yoff(dy) * 32 + 16 * rh, 16), n)
+
+    def three_tiles(k, dy):
+        top = part[k, block_rows(dy, 0, 16), :]
+        return [top[:, :128], top[:, 128:], part[k, block_rows(dy, 1, 16), :128]]
+
+    def fourth_tile(k, dy):
+        return part[k, block_rows(dy, 1, 16), 128:]
+
     for k, d in enumerate(FAR):
         cols = pl.ds(pl.multiple_of(zoff(d) * 256, 256), 256)
         both = jnp.dot(lhs[...], g_all[:, cols], preferred_element_type=f32)
         part[k] = both[:128] + both[128:]
+        if d:
+            message = za_send.at[d - 1]
+            scales = jnp.zeros((16, 128), f32)
+            for dy in range(NY):
+                tile = fourth_tile(k, dy)
+                scale = scale_of([tile])
+                message[dy] = encode([tile], scale)[0]
+                scales = jnp.where(row // 4 == dy, scale, scales)
+            message[4] = scales.astype(bf16)
+            remote(message, za_recv.at[d - 1], za_sent, za_came.at[d], at(zoff(d), y, c, x)).start()
         if k % 2 == 0:
             continue
         for dy in (2, 1, 3):
-            yy = yoff(dy)
-            message = y_send.at[k // 2, dy - 1]
+            message = yb_send.at[k // 2, dy - 1]
             scales = []
             for j in range(2):
-                tiles = tiles_of(part[k - 1 + j, pl.ds(pl.multiple_of(yy * 32, 32), 32), :])
+                tiles = three_tiles(k - 1 + j, dy)
                 scales.append(scale_of(tiles))
                 for i, code in enumerate(encode(tiles, scales[j])):
-                    message[4 * j + i] = code
-            message[8] = jnp.where(row < 8, scales[0], scales[1]).astype(bf16)
+                    message[3 * j + i] = code
+            message[6] = jnp.where(row < 8, scales[0], scales[1]).astype(bf16)
             remote(
-                message, y_recv.at[k // 2, dy - 1], ry_send, ry_recv.at[k // 2], at(z, yy, c, x)
+                message, yb_recv.at[k // 2, dy - 1], yb_sent, yb_came.at[k // 2], at(z, yoff(dy), c, x)
             ).start()
 
     sent(p_all.at[pl.ds(0, 480)], pz_send)
@@ -195,66 +218,126 @@
     for copy in pair:
         copy.wait_send()
 
-    own = pl.ds(pl.multiple_of(y * 32, 32), 32)
-    for k, d in enumerate(FAR):
+    def add(total, codes, scale):
+        return [a + b for a, b in zip(total, decode(codes, scale))]
+
+    def second_b(k, d):
         if k % 2 == 0:
-            arrived(y_recv.at[k // 2], ry_recv.at[k // 2])
-        total = tiles_of(part[k, own, :])
+            arrived(yb_recv.at[k // 2], yb_came.at[k // 2])
+        total = three_tiles(k, 0)
         for i in range(NY - 1):
-            message = y_recv.at[k // 2, i]
-            scale = message[8][8 * (k % 2) : 8 * (k % 2) + 1].astype(f32)
-            codes = [message[4 * (k % 2) + j] for j in range(4)]
-            total = [a + b for a, b in zip(total, decode(codes, scale))]
+            message = yb_recv.at[k // 2, i]
+            scale = message[6][8 * (k % 2) : 8 * (k % 2) + 1].astype(f32)
+            total = add(total, [message[3 * (k % 2) + j] for j in range(3)], scale)
         if d:
-            packet = z_send.at[d - 1]
+            message = zb_send.at[d - 1]
             scale = scale_of(total)
             for i, code in enumerate(encode(total, scale)):
-                packet[i] = code
-            packet[4] = jnp.broadcast_to(scale, (16, 128)).astype(bf16)
-            remote(packet, z_recv.at[d - 1], rz_send, rz_recv.at[d], at(zoff(d), y, c, x)).start()
-    sent(y_send, ry_send)
+                message[i] = code
+            message[3] = jnp.broadcast_to(scale, (16, 128)).astype(bf16)
+            remote(message, zb_recv.at[d - 1], zb_sent, zb_came.at[d], at(zoff(d), y, c, x)).start()
+        return total
+
+    for k in range(4):
+        second_b(k, FAR[k])
+    fourths = [fourth_tile(NZ - 1, dy) for dy in range(NY)]
     for d in NEAR[1:]:
-        packet = z_recv.at[d - 1]
-        arrived(packet, rz_recv.at[d])
-        codes = [packet[j] for j in range(4)]
-        total = [a + b for a, b in zip(total, decode(codes, packet[4][:1].astype(f32)))]
-
-    packet = gathered.at[c, z, y]
+        message = za_recv.at[d - 1]
+        arrived(message, za_came.at[d])
+        scales = message[4].astype(f32)
+        for dy in range(NY):
+            fourths[dy] = add([fourths[dy]], [message[dy]], scales[4 * dy : 4 * dy + 1])[0]
+    for dy in (2, 1, 3):
+        message = ya_send.at[dy - 1]
+        scale = scale_of([fourths[dy]])
+        message[0] = encode([fourths[dy]], scale)[0]
+        message[1] = jnp.broadcast_to(scale, (16, 128)).astype(bf16)
+        remote(message, ya_recv.at[dy - 1], ya_sent, ya_came, at(z, yoff(dy), c, x)).start()
+    for k in range(4, NZ):
+        total = second_b(k, FAR[k])
+    fourth = [fourths[0]]
+    arrived(ya_recv, ya_came)
+    for dy in range(1, NY):
+        message = ya_recv.at[dy - 1]
+        fourth = add(fourth, [message[0]], message[1][:1].astype(f32))
+    sent(yb_send, yb_sent)
+    sent(za_send, za_sent)
+    for d in NEAR[1:]:
+        message = zb_recv.at[d - 1]
+        arrived(message, zb_came.at[d])
+        total = add(total, [message[j] for j in range(3)], message[3][:1].astype(f32))
+    total = total + fourth
+
     scale = scale_of(total)
+    codes = encode(total, scale)
+    fourth_all[c, z, y] = codes[3]
+    for dy in (2, 1, 3):
+        block = fourth_all.at[c, z, y]
+        remote(block, block, by_sent, by_came, at(z, yoff(dy), c, x)).start()
     energy = jnp.sum(functools.reduce(jnp.add, [t * t for t in total]), axis=0, keepdims=True)
     e_high = energy.astype(bf16).astype(f32)
     e_mid = (energy - e_high).astype(bf16).astype(f32)
     e_low = energy - e_high - e_mid
-    for i, code in enumerate(encode(total, scale)):
-        packet[i] = code
     last = jnp.where(row < 8, scale, 0.0)
     for i, part_of in enumerate((e_high, e_mid, e_low)):
         last = jnp.where(row == 8 + i, part_of, last)
-    packet[4] = last.astype(bf16)
+    packet = column.at[z]
+    for i in range(3):
+        packet[i] = codes[i]
+    packet[3] = last.astype(bf16)
     for d in NEAR[:0:-1]:
-        remote(packet, packet, az_send, az_recv.at[d], at(zoff(d), y, c, x)).start()
+        remote(packet, packet, az_sent, az_came.at[d], at(zoff(d), y, c, x)).start()
 
     def out_forward(d):
-        block = gathered.at[c, zoff(NZ - d), y]
+        zz = zoff(NZ - d)
         if d:
-            arrived(block, az_recv.at[d])
+            arrived(column.at[zz], az_came.at[d])
+        block = column.at[zz, pl.ds(0, 3)]
         for dy in (2, 1, 3):
-            remote(block, block, ay_send, ay_recv.at[d], at(z, yoff(dy), c, x)).start()
+            remote(block, three_all.at[c, zz, y], ay_sent, ay_came.at[d], at(z, yoff(dy), c, x)).start()
+        three_all[c, zz, y] = column[zz, pl.ds(0, 3)]
 
     def out_share(d):
         zz = zoff(NZ - d)
-        arrived(gathered.at[c, zz, pl.ds(0, 3)], ay_recv.at[d])
-        remote(gathered.at[c, zz], gathered.at[c, zz], ac_send, ac_recv.at[d], sibling).start()
+        arrived(three_all.at[c, zz, pl.ds(0, 3)], ay_came.at[d])
+        if d:
+            arrived(fourth_all.at[c, zz], bz_came.at[d])
+        for ref in (three_all, fourth_all):
+            remote(ref.at[c, zz], ref.at[c, zz], ac_sent, ac_came.at[d], sibling).start()
 
     for k in range(NZ):
         out_forward(NEAR[k])
-    sent(z_send, rz_send)
-
-    tile = functools.reduce(jnp.add, [gathered[c, zz, y, 4].astype(f32) for zz in range(NZ)])
-    sums[0] = jnp.where(lax.broadcasted_iota(jnp.int32, (8, 128), 0) < 3, tile[8:], 0.0)
+        if k == 2:
+            arrived(fourth_all.at[c, z, pl.ds(0, 3)], by_came)
+            for d in NEAR[:0:-1]:
+                block = fourth_all.at[c, z]
+                remote(block, block, bz_sent, bz_came.at[d], at(zoff(d), y, c, x)).start()
+
+    tiles = [column[zz, 3].astype(f32) for zz in range(NZ)]
+    scales = functools.reduce(lambda a, b: jnp.where(row == b, tiles[b], a), range(1, NZ), tiles[0])
+    scale_all[c, y] = scales.astype(bf16)
+    for dy in (2, 1, 3):
+        block = scale_all.at[c, y]
+        remote(block, block, sy_sent, sy_came, at(z, yoff(dy), c, x)).start()
+    tile = functools.reduce(jnp.add, tiles)
+    sums[0] = jnp.where(row[:8] < 3, tile[8:], 0.0)
     for d in (2, 1, 3):
         remote(sums.at[0], sums.at[d], ex_send, ex_recv, at(z, y, c, xoff(d))).start()
-    for k in range(NZ // 2):
+    sent(zb_send, zb_sent)
+    sent(ya_send, ya_sent)
+
+    def widen(cc):
+        scale_wide[cc] = scale_all[cc].astype(f32)
+
+    def unpack(cc, zz):
+        for yy in range(NY):
+            codes = [three_all[cc, zz, yy, j] for j in range(3)] + [fourth_all[cc, zz, yy]]
+            for i, t in enumerate(decode(codes, scale_wide[cc, yy, pl.ds(zz, 1), :])):
+                rows = pl.ds(pl.multiple_of(cc * 128 + yy * 32 + (i // 2) * 16, 16), 16)
+                cols = pl.ds(pl.multiple_of(zz * 256 + (i % 2) * 128, 128), 128)
+                proj_out[rows, cols] = t
+
+    for k in range(3):
         out_share(NEAR[k])
     arrived(sums.at[pl.ds(0, 3)], ex_recv)
     sums[4] = sums[0] + sums[1] + sums[2] + sums[3]
@@ -265,35 +348,34 @@
                 cc = lax.rem(c + dc, 2)
                 remote(sums.at[4], sums.at[slot], ey_send, ey_recv, at(z, yoff(dy), cc, x)).start()
                 slot += 1
-    for k in range(NZ // 2, NZ):
+    arrived(scale_all.at[c, pl.ds(0, 3)], sy_came)
+    remote(scale_all.at[c], scale_all.at[c], sc_sent, sc_came, sibling).start()
+    widen(c)
+    for k in range(3, NZ):
         out_share(NEAR[k])
-
-    def unpack(cc, zz):
-        for yy in range(NY):
-            source = gathered.at[cc, zz, yy]
-            codes = [source[j] for j in range(4)]
-            for i, t in enumerate(decode(codes, source[4][:1].astype(f32))):
-                rows = pl.ds(pl.multiple_of(cc * 128 + yy * 32 + (i // 2) * 16, 16), 16)
-                cols = pl.ds(pl.multiple_of(zz * 256 + (i % 2) * 128, 128), 128)
-                proj_out[rows, cols] = t
-
-    def unpack_own(zz, carry):
-        unpack(c, zz)
-        return carry
-
-    lax.fori_loop(0, NZ, unpack_own, 0)
-    arrived(sums.at[pl.ds(0, 7)], ey_recv)
-    energy = functools.reduce(jnp.add, [sums[i] for i in range(4, 12)])
-    mean = jnp.full((8, 128), jnp.sum(energy) / entries + 1e-06, f32)
-    clip_out[...] = jnp.minimum(1.0, 1.0 / jnp.sqrt(mean))
-    for d in NEAR:
+        unpack(c, zoff(NZ - NEAR[k - 3]))
+    for k in range(NZ - 3, NZ):
+        unpack(c, zoff(NZ - NEAR[k]))
+    arrived(scale_all.at[1 - c], sc_came)
+    widen(1 - c)
+    for k, d in enumerate(NEAR):
         zz = zoff(NZ - d)
-        arrived(gathered.at[1 - c, zz], ac_recv.at[d])
+        arrived(fourth_all.at[0, pl.ds(0, 4)], ac_came.at[d])
         unpack(1 - c, zz)
-
-    sent(z_send, az_send)
-    sent(gathered.at[0, pl.ds(0, 6)], ay_send)
-    sent(gathered.at[0], ac_send)
+        if k == 3:
+            arrived(sums.at[pl.ds(0, 7)], ey_recv)
+            energy = functools.reduce(jnp.add, [sums[i] for i in range(4, 12)])
+            mean = jnp.full((8, 128), jnp.sum(energy) / entries + 1e-06, f32)
+            clip_out[...] = jnp.minimum(1.0, 1.0 / jnp.sqrt(mean))
+
+    sent(column.at[pl.ds(0, 7)], az_sent)
+    sent(three_all.at[0, pl.ds(0, 6)], ay_sent)
+    sent(fourth_all.at[0, 0, pl.ds(0, 3)], by_sent)
+    sent(fourth_all.at[0, pl.ds(0, 7)], bz_sent)
+    sent(scale_all.at[0, pl.ds(0, 3)], sy_sent)
+    sent(scale_all.at[0], sc_sent)
+    sent(fourth_all.at[0], ac_sent)
+    sent(three_all.at[0], ac_sent)
     sent(sums.at[pl.ds(0, 3)], ex_send)
     sent(sums.at[pl.ds(0, 7)], ey_send)
 
@@ -316,17 +398,25 @@
             pltpu.VMEM((1024, 128), f32),
             pltpu.VMEM((256, 1024), bf16),
             pltpu.VMEM((NZ, 128, 256), f32),
-            pltpu.VMEM((NZ // 2, NY - 1, 9, 16, 128), bf16),
-            pltpu.VMEM((NZ // 2, NY - 1, 9, 16, 128), bf16),
+            pltpu.VMEM((NZ // 2, NY - 1, 7, 16, 128), bf16),
+            pltpu.VMEM((NZ // 2, NY - 1, 7, 16, 128), bf16),
             pltpu.VMEM((NZ - 1, 5, 16, 128), bf16),
             pltpu.VMEM((NZ - 1, 5, 16, 128), bf16),
-            pltpu.VMEM((2, NZ, NY, 5, 16, 128), bf16),
+            pltpu.VMEM((NZ - 1, 4, 16, 128), bf16),
+            pltpu.VMEM((NZ - 1, 4, 16, 128), bf16),
+            pltpu.VMEM((NY - 1, 2, 16, 128), bf16),
+            pltpu.VMEM((NY - 1, 2, 16, 128), bf16),
+            pltpu.VMEM((NZ, 4, 16, 128), bf16),
+            pltpu.VMEM((2, NZ, NY, 3, 16, 128), bf16),
+            pltpu.VMEM((2, NZ, NY, 16, 128), bf16),
+            pltpu.VMEM((2, NY, 16, 128), bf16),
+            pltpu.VMEM((2, NY, 16, 128), f32),
             pltpu.VMEM((12, 8, 128), f32),
             sem((3,)), sem((2,)), sem((2,)),
             sem, sem((NZ,)), sem, sem((NZ,)),
-            sem, sem((NZ // 2,)), sem, sem((NZ,)),
-            sem, sem((NZ,)), sem, sem((NZ,)), sem, sem((NZ,)),
-            sem, sem, sem, sem,
+            sem, sem((NZ // 2,)), sem, sem((NZ,)), sem, sem((NZ,)), sem, sem,
+            sem, sem((NZ,)), sem, sem((NZ,)), sem, sem, sem, sem((NZ,)),
+            sem, sem, sem, sem, sem, sem((NZ,)), sem, sem, sem, sem,
         ],
         compiler_params=pltpu.CompilerParams(
             collective_id=0, has_side_effects=True, vmem_limit_bytes=20 * 1024 * 1024
@@ -342,23 +432,36 @@
     scale = jnp.concatenate([scale, scale], axis=1)
     rows = projector[...]
     copies = []
+
+    def start(src, dst, i, j):
+        cols = pl.ds(256 * i, 256)
+        copies.append(pltpu.make_async_copy(src.at[:, cols], dst.at[:, cols], sem.at[i, j]))
+        copies[-1].start()
+
+    def project(i, high, low):
+        moved = jnp.dot(rows, high, preferred_element_type=f32) + jnp.dot(rows, low, preferred_element_type=f32)
+        u_out[:, pl.ds(256 * i, 256)] = galore_scale * moved
+
+    waiting = None
     for i in range(8):
         cols = pl.ds(256 * i, 256)
+        if i:
+            project(i - 1, *waiting)
         clipped = scale * proj[:, cols]
         first = beta_one * first_old[:, cols] + (1.0 - beta_one) * clipped
         second = beta_two * second_old[:, cols] + (1.0 - beta_two) * clipped * clipped
         f_out[:, cols] = first
         s_out[:, cols] = second
-        for j, (src, dst) in enumerate(((f_out, first_new), (s_out, second_new))):
-            copies.append(pltpu.make_async_copy(src.at[:, cols], dst.at[:, cols], sem.at[i, j]))
-            copies[-1].start()
-        direction = first * (1.0 / bias_one) / (jnp.sqrt(second * (1.0 / bias_two)) + 1e-08)
+        square = second * (1.0 / bias_two)
+        direction = first * (1.0 / bias_one) / (square * lax.rsqrt(square) + 1e-08)
         high = direction.astype(bf16)
-        low = (direction - high.astype(f32)).astype(bf16)
-        moved = jnp.dot(rows, high, preferred_element_type=f32) + jnp.dot(rows, low, preferred_element_type=f32)
-        u_out[:, cols] = galore_scale * moved
-        copies.append(pltpu.make_async_copy(u_out.at[:, cols], update.at[:, cols], sem.at[i, 2]))
-        copies[-1].start()
+        waiting = (high, (direction - high.astype(f32)).astype(bf16))
+        start(f_out, first_new, i, 0)
+        start(s_out, second_new, i, 1)
+        if i:
+            start(u_out, update, i - 1, 2)
+    project(7, *waiting)
+    start(u_out, update, 7, 2)
     for copy in copies:
         copy.wait()
 

time: 54.1 us -> 53.5 us (0.989)
    pallas_call x1, Pallas kernels: 3.76 us -> 3.17 us  [updated(): pl.pallas_call(update_kernel, name='adam_update', out_shape=(jax.ShapeDty...]
where the time goes in v3:
time: 53.5 us
  Pallas kernels  52.8 us (99%)
  between operations  0.69 us (1%)
    pallas_call x1, Pallas kernels, reduced(): pl.pallas_call(functools.partial(reduce_kernel, entries), name='projected...  49.6 us
    pallas_call x1, Pallas kernels, updated(): pl.pallas_call(update_kernel, name='adam_update', out_shape=(jax.ShapeDty...  3.17 us

profile of v3, /device:TPU:1, one launch (start us, length us, event | category | flops | bytes accessed | tf_op | source)
XLA Modules:
  0.0 53.5 jit_solution(5944804993627992848)
XLA Ops:
  0.6 0.0 copy-start.2
  0.6 0.0 copy-start.1
  0.7 0.0 copy-start
  0.7 49.6 %projected_gradient.1 = (f32[256,2048]{1,0:T(8,128)S(1)}, f32[8,128]{1,0:T(8,128)S(1)}) custom-call(bf16[512,2048]{1,0:T(8,128)(2,1)} %acts.1, bf16[512,2048]{1,0:T(8,128)(2,1)} %grad.1, bf16[32,256]{1,0:T(8,128)(2,1)} %projector.1), custom_call_target="tpu_custom_call" | custom-call | flops 2147483648 | bytes 6291456 | tf_op jit(solution)/shard_map/projected_gradient/pallas_call | solution.py:387
  50.2 0.0 copy-done.2
  50.3 0.0 copy-done.1
  50.3 0.0 copy-done
  50.3 3.2 %adam_update.1 = (f32[32,2048]{1,0:T(8,128)}, f32[256,2048]{1,0:T(8,128)}, f32[256,2048]{1,0:T(8,128)}) custom-call(f32[256,2048]{1,0:T(8,128)S(1)} %get-tuple-element.5.proj, f32[8,128]{1,0:T(8,128)S(1)} %get-tuple-element.6.clip, bf16[32,256]{1,0:T(8,128)(2,1)S(1)} %copy-done.2, f32[256,2048]{1,0:T(8,128)S(1)} %copy-done, f32[256,2048]{1,0:T(8,128)S(1)} %copy-done.1), custom_call_target="tpu_custom_call" | custom-call | flops 67108864 | bytes 10485760 | tf_op jit(solution)/shard_map/adam_update/pallas_call | solution.py:472
Async XLA Ops:
  0.6 49.6 %copy-start.2 = (bf16[32,256]{1,0:T(8,128)(2,1)S(1)}, bf16[32,256]{1,0:T(8,128)(2,1)}, u32[]{:S(2)}) copy-start(bf16[32,256]{1,0:T(8,128)(2,1)} %projector.1) | copy-start | bytes 49156
  0.6 49.6 %copy-start.1 = (f32[256,2048]{1,0:T(8,128)S(1)}, f32[256,2048]{1,0:T(8,128)}, u32[]{:S(2)}) copy-start(f32[256,2048]{1,0:T(8,128)} %second_old.1) | copy-start | bytes 6291460
  0.7 49.6 %copy-start = (f32[256,2048]{1,0:T(8,128)S(1)}, f32[256,2048]{1,0:T(8,128)}, u32[]{:S(2)}) copy-start(f32[256,2048]{1,0:T(8,128)} %first_old.1) | copy-start | bytes 6291460

commit v4 on v2

--- a/solution.py
+++ b/solution.py
@@ -56,10 +56,12 @@
 
 def reduce_kernel(
     entries, acts, grad, p_hbm, proj_out, clip_out,
-    p_ref, a_all, g_all, p_all, along, lhs, part, y_send, y_recv, z_send, z_recv, gathered, sums,
+    p_ref, a_all, g_all, p_all, along, lhs, part,
+    yb_send, yb_recv, zb_send, zb_recv, column, blocks, scale_all, scale_wide, sums,
     load_sem, pair_send, pair_recv, pz_send, pz_recv, py_send, py_recv,
-    ry_send, ry_recv, rz_send, rz_recv, az_send, az_recv, ay_send, ay_recv, ac_send, ac_recv,
-    ex_send, ex_recv, ey_send, ey_recv,
+    yb_sent, yb_came, zb_sent, zb_came, az_sent, az_came, ay_sent, ay_came,
+    sy_sent, sy_came, sc_sent, sc_came, ac_sent, ac_came,
+    ex_send, ex_recv, ez_send, ez_recv, ey_send, ey_recv,
 ):
     dp = lax.axis_index("dp")
     x = lax.axis_index("group")
@@ -121,7 +123,7 @@
         def _():
             p_all[mine, :] = p_ref[:, cc * 128 : cc * 128 + 128]
 
-    for d in NEAR[:0:-1]:
+    for d in NEAR[1:]:
         for cc in range(2):
             src = p_ref.at[:, pl.ds(cc * 128, 128)]
             remote(src, p_all.at[mine], pz_send, pz_recv.at[d], at(zoff(d), y, cc, x)).start()
@@ -170,24 +172,35 @@
     pair[1].wait_recv()
 
     row = lax.broadcasted_iota(jnp.int32, (16, 128), 0)
-    for k, d in enumerate(FAR):
-        cols = pl.ds(pl.multiple_of(zoff(d) * 256, 256), 256)
-        both = jnp.dot(lhs[...], g_all[:, cols], preferred_element_type=f32)
-        part[k] = both[:128] + both[128:]
-        if k % 2 == 0:
-            continue
+
+    def four_tiles(k, dy):
+        return tiles_of(part[k, pl.ds(pl.multiple_of(yoff(dy) * 32, 32), 32), :])
+
+    def multiply(p):
+        for k in (2 * p, 2 * p + 1):
+            cols = pl.ds(pl.multiple_of(zoff(FAR[k]) * 256, 256), 256)
+            both = jnp.dot(lhs[...], g_all[:, cols], preferred_element_type=f32)
+            part[k] = both[:128] + both[128:]
+
+    def first_b(p, dy):
+        message = yb_send.at[p, dy - 1]
+        scales = []
+        for j in range(2):
+            tiles = four_tiles(2 * p + j, dy)
+            scales.append(scale_of(tiles))
+            for i, code in enumerate(encode(tiles, scales[j])):
+                message[4 * j + i] = code
+        message[8] = jnp.where(row < 8, scales[0], scales[1]).astype(bf16)
+
+    multiply(0)
+    for p in range(NZ // 2):
+        if p < NZ // 2 - 1:
+            multiply(p + 1)
         for dy in (2, 1, 3):
-            yy = yoff(dy)
-            message = y_send.at[k // 2, dy - 1]
-            scales = []
-            for j in range(2):
-                tiles = tiles_of(part[k - 1 + j, pl.ds(pl.multiple_of(yy * 32, 32), 32), :])
-                scales.append(scale_of(tiles))
-                for i, code in enumerate(encode(tiles, scales[j])):
-                    message[4 * j + i] = code
-            message[8] = jnp.where(row < 8, scales[0], scales[1]).astype(bf16)
+            first_b(p, dy)
+        for dy in (2, 1, 3):
             remote(
-                message, y_recv.at[k // 2, dy - 1], ry_send, ry_recv.at[k // 2], at(z, yy, c, x)
+                yb_send.at[p, dy - 1], yb_recv.at[p, dy - 1], yb_sent, yb_came.at[p], at(z, yoff(dy), c, x)
             ).start()
 
     sent(p_all.at[pl.ds(0, 480)], pz_send)
@@ -195,106 +208,138 @@
     for copy in pair:
         copy.wait_send()
 
-    own = pl.ds(pl.multiple_of(y * 32, 32), 32)
-    for k, d in enumerate(FAR):
-        if k % 2 == 0:
-            arrived(y_recv.at[k // 2], ry_recv.at[k // 2])
-        total = tiles_of(part[k, own, :])
-        for i in range(NY - 1):
-            message = y_recv.at[k // 2, i]
-            scale = message[8][8 * (k % 2) : 8 * (k % 2) + 1].astype(f32)
-            codes = [message[4 * (k % 2) + j] for j in range(4)]
-            total = [a + b for a, b in zip(total, decode(codes, scale))]
-        if d:
-            packet = z_send.at[d - 1]
-            scale = scale_of(total)
-            for i, code in enumerate(encode(total, scale)):
-                packet[i] = code
-            packet[4] = jnp.broadcast_to(scale, (16, 128)).astype(bf16)
-            remote(packet, z_recv.at[d - 1], rz_send, rz_recv.at[d], at(zoff(d), y, c, x)).start()
-    sent(y_send, ry_send)
+    def add(total, codes, scale):
+        return [a + b for a, b in zip(total, decode(codes, scale))]
+
+    def second_b(p):
+        arrived(yb_recv.at[p], yb_came.at[p])
+        for j, d in enumerate((FAR[2 * p], FAR[2 * p + 1])):
+            total = four_tiles(2 * p + j, 0)
+            for i in range(NY - 1):
+                message = yb_recv.at[p, i]
+                scale = message[8][8 * j : 8 * j + 1].astype(f32)
+                total = add(total, [message[4 * j + t] for t in range(4)], scale)
+            if d:
+                message = zb_send.at[d - 1]
+                scale = scale_of(total)
+                for i, code in enumerate(encode(total, scale)):
+                    message[i] = code
+                message[4] = jnp.broadcast_to(scale, (16, 128)).astype(bf16)
+        for d in (FAR[2 * p], FAR[2 * p + 1]):
+            if d:
+                remote(
+                    zb_send.at[d - 1], zb_recv.at[d - 1], zb_sent, zb_came.at[d], at(zoff(d), y, c, x)
+                ).start()
+        return total
+
+    for p in range(NZ // 2):
+        total = second_b(p)
+    sent(yb_send, yb_sent)
     for d in NEAR[1:]:
-        packet = z_recv.at[d - 1]
-        arrived(packet, rz_recv.at[d])
-        codes = [packet[j] for j in range(4)]
-        total = [a + b for a, b in zip(total, decode(codes, packet[4][:1].astype(f32)))]
-
-    packet = gathered.at[c, z, y]
+        message = zb_recv.at[d - 1]
+        arrived(message, zb_came.at[d])
+        total = add(total, [message[j] for j in range(4)], message[4][:1].astype(f32))
+
+    square = functools.reduce(jnp.add, [t * t for t in total])
+    sums[0] = square[:8] + square[8:]
     scale = scale_of(total)
-    energy = jnp.sum(functools.reduce(jnp.add, [t * t for t in total]), axis=0, keepdims=True)
-    e_high = energy.astype(bf16).astype(f32)
-    e_mid = (energy - e_high).astype(bf16).astype(f32)
-    e_low = energy - e_high - e_mid
+    packet = column.at[z]
     for i, code in enumerate(encode(total, scale)):
         packet[i] = code
-    last = jnp.where(row < 8, scale, 0.0)
-    for i, part_of in enumerate((e_high, e_mid, e_low)):
-        last = jnp.where(row == 8 + i, part_of, last)
-    packet[4] = last.astype(bf16)
-    for d in NEAR[:0:-1]:
-        remote(packet, packet, az_send, az_recv.at[d], at(zoff(d), y, c, x)).start()
+    packet[4] = jnp.broadcast_to(scale, (16, 128)).astype(bf16)
+    for d in (2, 1, 3):
+        remote(sums.at[0], sums.at[d], ex_send, ex_recv, at(z, y, c, xoff(d))).start()
+    for d in NEAR[1:]:
+        remote(packet, packet, az_sent, az_came.at[d], at(zoff(d), y, c, x)).start()
 
     def out_forward(d):
-        block = gathered.at[c, zoff(NZ - d), y]
+        zz = zoff(NZ - d)
         if d:
-            arrived(block, az_recv.at[d])
+            arrived(column.at[zz], az_came.at[d])
+        block = column.at[zz, pl.ds(0, 4)]
         for dy in (2, 1, 3):
-            remote(block, block, ay_send, ay_recv.at[d], at(z, yoff(dy), c, x)).start()
+            remote(block, blocks.at[c, zz, y], ay_sent, ay_came.at[d], at(z, yoff(dy), c, x)).start()
+        blocks[c, zz, y] = column[zz, pl.ds(0, 4)]
 
     def out_share(d):
-        zz = zoff(NZ - d)
-        arrived(gathered.at[c, zz, pl.ds(0, 3)], ay_recv.at[d])
-        remote(gathered.at[c, zz], gathered.at[c, zz], ac_send, ac_recv.at[d], sibling).start()
+        block = blocks.at[c, zoff(NZ - d)]
+        arrived(blocks.at[c, zoff(NZ - d), pl.ds(0, 3)], ay_came.at[d])
+        remote(block, block, ac_sent, ac_came.at[d], sibling).start()
 
     for k in range(NZ):
         out_forward(NEAR[k])
-    sent(z_send, rz_send)
-
-    tile = functools.reduce(jnp.add, [gathered[c, zz, y, 4].astype(f32) for zz in range(NZ)])
-    sums[0] = jnp.where(lax.broadcasted_iota(jnp.int32, (8, 128), 0) < 3, tile[8:], 0.0)
-    for d in (2, 1, 3):
-        remote(sums.at[0], sums.at[d], ex_send, ex_recv, at(z, y, c, xoff(d))).start()
-    for k in range(NZ // 2):
-        out_share(NEAR[k])
-    arrived(sums.at[pl.ds(0, 3)], ex_recv)
-    sums[4] = sums[0] + sums[1] + sums[2] + sums[3]
-    slot = 5
+        if k == 2:
+            arrived(sums.at[pl.ds(0, 3)], ex_recv)
+            sums[4] = sums[0] + sums[1] + sums[2] + sums[3]
+            for d in NEAR[:0:-1]:
+                remote(sums.at[4], sums.at[4 + d], ez_send, ez_recv, at(zoff(d), y, c, x)).start()
+
+    tiles = [column[zz, 4] for zz in range(NZ)]
+    scale_all[c, y] = functools.reduce(lambda a, b: jnp.where(row == b, tiles[b], a), range(1, NZ), tiles[0])
+    for dy in (2, 1, 3):
+        block = scale_all.at[c, y]
+        remote(block, block, sy_sent, sy_came, at(z, yoff(dy), c, x)).start()
+    arrived(sums.at[pl.ds(0, 7)], ez_recv)
+    sums[12] = functools.reduce(jnp.add, [sums[i] for i in range(4, 12)])
+    slot = 13
     for dy in (2, 1, 3, 0):
         for dc in (1, 0):
             if dy or dc:
                 cc = lax.rem(c + dc, 2)
-                remote(sums.at[4], sums.at[slot], ey_send, ey_recv, at(z, yoff(dy), cc, x)).start()
+                remote(sums.at[12], sums.at[slot], ey_send, ey_recv, at(z, yoff(dy), cc, x)).start()
                 slot += 1
-    for k in range(NZ // 2, NZ):
-        out_share(NEAR[k])
+    sent(zb_send, zb_sent)
+
+    def widen(cc):
+        scale_wide[cc] = scale_all[cc].astype(f32)
 
     def unpack(cc, zz):
         for yy in range(NY):
-            source = gathered.at[cc, zz, yy]
-            codes = [source[j] for j in range(4)]
-            for i, t in enumerate(decode(codes, source[4][:1].astype(f32))):
+            codes = [blocks[cc, zz, yy, j] for j in range(4)]
+            for i, t in enumerate(decode(codes, scale_wide[cc, yy, pl.ds(zz, 1), :])):
                 rows = pl.ds(pl.multiple_of(cc * 128 + yy * 32 + (i // 2) * 16, 16), 16)
                 cols = pl.ds(pl.multiple_of(zz * 256 + (i % 2) * 128, 128), 128)
                 proj_out[rows, cols] = t
 
-    def unpack_own(zz, carry):
-        unpack(c, zz)
+    def near(k):
+        return lax.rem(jnp.where(lax.rem(k, 2) == 1, lax.div(k + 1, 2), NZ - lax.div(k, 2)), NZ)
+
+    def unpack_own(k, carry):
+        unpack(c, zoff(NZ - near(k)))
         return carry
 
-    lax.fori_loop(0, NZ, unpack_own, 0)
+    def unpack_theirs(k, carry):
+        d = near(k)
+        zz = zoff(NZ - d)
+        arrived(blocks.at[1 - c, zz], ac_came.at[d])
+        unpack(1 - c, zz)
+        return carry
+
+    for k in range(NZ - 2):
+        out_share(NEAR[k])
+    arrived(scale_all.at[c, pl.ds(0, 3)], sy_came)
+    remote(scale_all.at[c], scale_all.at[c], sc_sent, sc_came, sibling).start()
+    widen(c)
+    lax.fori_loop(0, NZ // 2, unpack_own, 0)
+    for k in range(NZ - 2, NZ):
+        out_share(NEAR[k])
+    lax.fori_loop(NZ // 2, NZ, unpack_own, 0)
+    arrived(scale_all.at[1 - c], sc_came)
+    widen(1 - c)
+    lax.fori_loop(0, NZ - 2, unpack_theirs, 0)
     arrived(sums.at[pl.ds(0, 7)], ey_recv)
-    energy = functools.reduce(jnp.add, [sums[i] for i in range(4, 12)])
+    energy = functools.reduce(jnp.add, [sums[i] for i in range(12, 20)])
     mean = jnp.full((8, 128), jnp.sum(energy) / entries + 1e-06, f32)
     clip_out[...] = jnp.minimum(1.0, 1.0 / jnp.sqrt(mean))
-    for d in NEAR:
-        zz = zoff(NZ - d)
-        arrived(gathered.at[1 - c, zz], ac_recv.at[d])
-        unpack(1 - c, zz)
-
-    sent(z_send, az_send)
-    sent(gathered.at[0, pl.ds(0, 6)], ay_send)
-    sent(gathered.at[0], ac_send)
+    lax.fori_loop(NZ - 2, NZ, unpack_theirs, 0)
+
+    sent(column.at[pl.ds(0, 7)], az_sent)
+    sent(blocks.at[0, pl.ds(0, 6)], ay_sent)
+    sent(scale_all.at[0, pl.ds(0, 3)], sy_sent)
+    sent(scale_all.at[0], sc_sent)
+    sent(blocks.at[0], ac_sent)
     sent(sums.at[pl.ds(0, 3)], ex_send)
+    sent(sums.at[pl.ds(0, 7)], ez_send)
     sent(sums.at[pl.ds(0, 7)], ey_send)
 
 
@@ -320,13 +365,15 @@
             pltpu.VMEM((NZ // 2, NY - 1, 9, 16, 128), bf16),
             pltpu.VMEM((NZ - 1, 5, 16, 128), bf16),
             pltpu.VMEM((NZ - 1, 5, 16, 128), bf16),
-            pltpu.VMEM((2, NZ, NY, 5, 16, 128), bf16),
-            pltpu.VMEM((12, 8, 128), f32),
-            sem((3,)), sem((2,)), sem((2,)),
-            sem, sem((NZ,)), sem, sem((NZ,)),
-            sem, sem((NZ // 2,)), sem, sem((NZ,)),
-            sem, sem((NZ,)), sem, sem((NZ,)), sem, sem((NZ,)),
-            sem, sem, sem, sem,
+            pltpu.VMEM((NZ, 5, 16, 128), bf16),
+            pltpu.VMEM((2, NZ, NY, 4, 16, 128), bf16),
+            pltpu.VMEM((2, NY, 16, 128), bf16),
+            pltpu.VMEM((2, NY, 16, 128), f32),
+            pltpu.VMEM((20, 8, 128), f32),
+            sem((3,)), sem((2,)), sem((2,)), sem, sem((NZ,)), sem, sem((NZ,)),
+            sem, sem((NZ // 2,)), sem, sem((NZ,)), sem, sem((NZ,)), sem, sem((NZ,)),
+            sem, sem, sem, sem, sem, sem((NZ,)),
+            sem, sem, sem, sem, sem, sem,
         ],
         compiler_params=pltpu.CompilerParams(
             collective_id=0, has_side_effects=True, vmem_limit_bytes=20 * 1024 * 1024
@@ -342,23 +389,36 @@
     scale = jnp.concatenate([scale, scale], axis=1)
     rows = projector[...]
     copies = []
+
+    def start(src, dst, i, j):
+        cols = pl.ds(256 * i, 256)
+        copies.append(pltpu.make_async_copy(src.at[:, cols], dst.at[:, cols], sem.at[i, j]))
+        copies[-1].start()
+
+    def project(i, high, low):
+        moved = jnp.dot(rows, high, preferred_element_type=f32) + jnp.dot(rows, low, preferred_element_type=f32)
+        u_out[:, pl.ds(256 * i, 256)] = galore_scale * moved
+
+    waiting = None
     for i in range(8):
         cols = pl.ds(256 * i, 256)
+        if i:
+            project(i - 1, *waiting)
         clipped = scale * proj[:, cols]
         first = beta_one * first_old[:, cols] + (1.0 - beta_one) * clipped
         second = beta_two * second_old[:, cols] + (1.0 - beta_two) * clipped * clipped
         f_out[:, cols] = first
         s_out[:, cols] = second
-        for j, (src, dst) in enumerate(((f_out, first_new), (s_out, second_new))):
-            copies.append(pltpu.make_async_copy(src.at[:, cols], dst.at[:, cols], sem.at[i, j]))
-            copies[-1].start()
-        direction = first * (1.0 / bias_one) / (jnp.sqrt(second * (1.0 / bias_two)) + 1e-08)
+        square = second * (1.0 / bias_two)
+        direction = first * (1.0 / bias_one) / (square * lax.rsqrt(square) + 1e-08)
         high = direction.astype(bf16)
-        low = (direction - high.astype(f32)).astype(bf16)
-        moved = jnp.dot(rows, high, preferred_element_type=f32) + jnp.dot(rows, low, preferred_element_type=f32)
-        u_out[:, cols] = galore_scale * moved
-        copies.append(pltpu.make_async_copy(u_out.at[:, cols], update.at[:, cols], sem.at[i, 2]))
-        copies[-1].start()
+        waiting = (high, (direction - high.astype(f32)).astype(bf16))
+        start(f_out, first_new, i, 0)
+        start(s_out, second_new, i, 1)
+        if i:
+            start(u_out, update, i - 1, 2)
+    project(7, *waiting)
+    start(u_out, update, 7, 2)
     for copy in copies:
         copy.wait()
 

time: 54.1 us -> 51.1 us (0.945)
  Pallas kernels: 53.3 us -> 50.4 us
    pallas_call x1, Pallas kernels: 49.6 us -> 47.2 us  [reduced(): pl.pallas_call(functools.partial(reduce_kernel, entries), name='projected...]
    pallas_call x1, Pallas kernels: 3.76 us -> 3.17 us  [updated(): pl.pallas_call(update_kernel, name='adam_update', out_shape=(jax.ShapeDty...]
where the time goes in v4:
time: 51.1 us; the launch traced here: 51 us
  Pallas kernels  50.4 us (99%)
  between operations  0.69 us (1%)
    pallas_call x1, Pallas kernels, reduced(): pl.pallas_call(functools.partial(reduce_kernel, entries), name='projected...  47.2 us
    pallas_call x1, Pallas kernels, updated(): pl.pallas_call(update_kernel, name='adam_update', out_shape=(jax.ShapeDty...  3.17 us

profile of v4, /device:TPU:1, one launch (start us, length us, event | category | flops | bytes accessed | tf_op | source)
XLA Modules:
  0.0 51.0 jit_solution(12215677822070057403)
XLA Ops:
  0.6 0.0 copy-start.2
  0.6 0.0 copy-start.1
  0.7 0.0 copy-start
  0.7 47.2 %projected_gradient.1 = (f32[256,2048]{1,0:T(8,128)S(1)}, f32[8,128]{1,0:T(8,128)S(1)}) custom-call(bf16[512,2048]{1,0:T(8,128)(2,1)} %acts.1, bf16[512,2048]{1,0:T(8,128)(2,1)} %grad.1, bf16[32,256]{1,0:T(8,128)(2,1)} %projector.1), custom_call_target="tpu_custom_call" | custom-call | flops 2147483648 | bytes 6291456 | tf_op jit(solution)/shard_map/projected_gradient/pallas_call | solution.py:350
  47.8 0.0 copy-done.2
  47.9 0.0 copy-done.1
  47.9 0.0 copy-done
  47.9 3.2 %adam_update.1 = (f32[32,2048]{1,0:T(8,128)}, f32[256,2048]{1,0:T(8,128)}, f32[256,2048]{1,0:T(8,128)}) custom-call(f32[256,2048]{1,0:T(8,128)S(1)} %get-tuple-element.5.proj, f32[8,128]{1,0:T(8,128)S(1)} %get-tuple-element.6.clip, bf16[32,256]{1,0:T(8,128)(2,1)S(1)} %copy-done.2, f32[256,2048]{1,0:T(8,128)S(1)} %copy-done, f32[256,2048]{1,0:T(8,128)S(1)} %copy-done.1), custom_call_target="tpu_custom_call" | custom-call | flops 67108864 | bytes 10485760 | tf_op jit(solution)/shard_map/adam_update/pallas_call | solution.py:429
Async XLA Ops:
  0.6 47.2 %copy-start.2 = (bf16[32,256]{1,0:T(8,128)(2,1)S(1)}, bf16[32,256]{1,0:T(8,128)(2,1)}, u32[]{:S(2)}) copy-start(bf16[32,256]{1,0:T(8,128)(2,1)} %projector.1) | copy-start | bytes 49156
  0.6 47.2 %copy-start.1 = (f32[256,2048]{1,0:T(8,128)S(1)}, f32[256,2048]{1,0:T(8,128)}, u32[]{:S(2)}) copy-start(f32[256,2048]{1,0:T(8,128)} %second_old.1) | copy-start | bytes 6291460
  0.7 47.2 %copy-start = (f32[256,2048]{1,0:T(8,128)S(1)}, f32[256,2048]{1,0:T(8,128)}, u32[]{:S(2)}) copy-start(f32[256,2048]{1,0:T(8,128)} %first_old.1) | copy-start | bytes 6291460

commit v5 on v4

--- a/solution.py
+++ b/solution.py
@@ -57,9 +57,9 @@
 def reduce_kernel(
     entries, acts, grad, p_hbm, proj_out, clip_out,
     p_ref, a_all, g_all, p_all, along, lhs, part,
-    yb_send, yb_recv, zb_send, zb_recv, column, blocks, scale_all, scale_wide, sums,
+    yb_send, yb_recv, ys_send, ys_recv, zb_send, zb_recv, column, blocks, scale_all, scale_wide, sums,
     load_sem, pair_send, pair_recv, pz_send, pz_recv, py_send, py_recv,
-    yb_sent, yb_came, zb_sent, zb_came, az_sent, az_came, ay_sent, ay_came,
+    yb_sent, yb_came, ys_sent, ys_came, zb_sent, zb_came, az_sent, az_came, ay_sent, ay_came,
     sy_sent, sy_came, sc_sent, sc_came, ac_sent, ac_came,
     ex_send, ex_recv, ez_send, ez_recv, ey_send, ey_recv,
 ):
@@ -151,7 +151,9 @@
             loads[1].wait()
             pair[0].wait_recv()
         cols = pl.ds(pl.multiple_of(zz * 256, 256), 256)
-        term = jnp.dot(a_all[:, cols], p_all[p_rows(zz, 0, 256), :], preferred_element_type=f32)
+        term = lax.dot_general(
+            p_all[p_rows(zz, 0, 256), :], a_all[:, cols], (((0,), (1,)), ((), ())), preferred_element_type=f32
+        )
         if first:
             along[...] = term
         else:
@@ -164,7 +166,7 @@
         if k >= lag:
             p_use(NEAR[k - lag], k == lag)
 
-    turned = along[...].T
+    turned = along[...]
     high = turned.astype(bf16)
     lhs[pl.ds(0, 128), :] = high
     lhs[pl.ds(128, 128), :] = (turned - high.astype(f32)).astype(bf16)
@@ -176,32 +178,25 @@
     def four_tiles(k, dy):
         return tiles_of(part[k, pl.ds(pl.multiple_of(yoff(dy) * 32, 32), 32), :])
 
-    def multiply(p):
-        for k in (2 * p, 2 * p + 1):
-            cols = pl.ds(pl.multiple_of(zoff(FAR[k]) * 256, 256), 256)
-            both = jnp.dot(lhs[...], g_all[:, cols], preferred_element_type=f32)
-            part[k] = both[:128] + both[128:]
-
-    def first_b(p, dy):
-        message = yb_send.at[p, dy - 1]
-        scales = []
-        for j in range(2):
-            tiles = four_tiles(2 * p + j, dy)
-            scales.append(scale_of(tiles))
-            for i, code in enumerate(encode(tiles, scales[j])):
-                message[4 * j + i] = code
-        message[8] = jnp.where(row < 8, scales[0], scales[1]).astype(bf16)
+    def multiply(k):
+        cols = pl.ds(pl.multiple_of(zoff(FAR[k]) * 256, 256), 256)
+        both = jnp.dot(lhs[...], g_all[:, cols], preferred_element_type=f32)
+        part[k] = both[:128] + both[128:]
 
     multiply(0)
-    for p in range(NZ // 2):
-        if p < NZ // 2 - 1:
-            multiply(p + 1)
+    for k in range(NZ):
+        if k < NZ - 1:
+            multiply(k + 1)
         for dy in (2, 1, 3):
-            first_b(p, dy)
+            tiles = four_tiles(k, dy)
+            scale = scale_of(tiles)
+            for i, code in enumerate(encode(tiles, scale)):
+                yb_send[k, dy - 1, i] = code
+            ys_send[k, dy - 1] = scale
         for dy in (2, 1, 3):
-            remote(
-                yb_send.at[p, dy - 1], yb_recv.at[p, dy - 1], yb_sent, yb_came.at[p], at(z, yoff(dy), c, x)
-            ).start()
+            there = at(z, yoff(dy), c, x)
+            remote(yb_send.at[k, dy - 1], yb_recv.at[k, dy - 1], yb_sent, yb_came.at[k], there).start()
+            remote(ys_send.at[k, dy - 1], ys_recv.at[k, dy - 1], ys_sent, ys_came.at[k], there).start()
 
     sent(p_all.at[pl.ds(0, 480)], pz_send)
     sent(p_all.at[pl.ds(0, 1536)], py_send)
@@ -211,30 +206,21 @@
     def add(total, codes, scale):
         return [a + b for a, b in zip(total, decode(codes, scale))]
 
-    def second_b(p):
-        arrived(yb_recv.at[p], yb_came.at[p])
-        for j, d in enumerate((FAR[2 * p], FAR[2 * p + 1])):
-            total = four_tiles(2 * p + j, 0)
-            for i in range(NY - 1):
-                message = yb_recv.at[p, i]
-                scale = message[8][8 * j : 8 * j + 1].astype(f32)
-                total = add(total, [message[4 * j + t] for t in range(4)], scale)
-            if d:
-                message = zb_send.at[d - 1]
-                scale = scale_of(total)
-                for i, code in enumerate(encode(total, scale)):
-                    message[i] = code
-                message[4] = jnp.broadcast_to(scale, (16, 128)).astype(bf16)
-        for d in (FAR[2 * p], FAR[2 * p + 1]):
-            if d:
-                remote(
-                    zb_send.at[d - 1], zb_recv.at[d - 1], zb_sent, zb_came.at[d], at(zoff(d), y, c, x)
-                ).start()
-        return total
-
-    for p in range(NZ // 2):
-        total = second_b(p)
+    for k, d in enumerate(FAR):
+        arrived(yb_recv.at[k], yb_came.at[k])
+        arrived(ys_recv.at[k], ys_came.at[k])
+        total = four_tiles(k, 0)
+        for i in range(NY - 1):
+            total = add(total, [yb_recv[k, i, j] for j in range(4)], ys_recv[k, i])
+        if d:
+            message = zb_send.at[d - 1]
+            scale = scale_of(total)
+            for i, code in enumerate(encode(total, scale)):
+                message[i] = code
+            message[4] = jnp.broadcast_to(scale, (16, 128)).astype(bf16)
+            remote(message, zb_recv.at[d - 1], zb_sent, zb_came.at[d], at(zoff(d), y, c, x)).start()
     sent(yb_send, yb_sent)
+    sent(ys_send, ys_sent)
     for d in NEAR[1:]:
         message = zb_recv.at[d - 1]
         arrived(message, zb_came.at[d])
@@ -358,11 +344,13 @@
             pltpu.VMEM((1024, 2048), bf16),
             pltpu.VMEM((1024, 2048), bf16),
             pltpu.VMEM((2048, 128), bf16),
-            pltpu.VMEM((1024, 128), f32),
+            pltpu.VMEM((128, 1024), f32),
             pltpu.VMEM((256, 1024), bf16),
             pltpu.VMEM((NZ, 128, 256), f32),
-            pltpu.VMEM((NZ // 2, NY - 1, 9, 16, 128), bf16),
-            pltpu.VMEM((NZ // 2, NY - 1, 9, 16, 128), bf16),
+            pltpu.VMEM((NZ, NY - 1, 4, 16, 128), bf16),
+            pltpu.VMEM((NZ, NY - 1, 4, 16, 128), bf16),
+            pltpu.VMEM((NZ, NY - 1, 1, 128), f32),
+            pltpu.VMEM((NZ, NY - 1, 1, 128), f32),
             pltpu.VMEM((NZ - 1, 5, 16, 128), bf16),
             pltpu.VMEM((NZ - 1, 5, 16, 128), bf16),
             pltpu.VMEM((NZ, 5, 16, 128), bf16),
@@ -371,7 +359,7 @@
             pltpu.VMEM((2, NY, 16, 128), f32),
             pltpu.VMEM((20, 8, 128), f32),
             sem((3,)), sem((2,)), sem((2,)), sem, sem((NZ,)), sem, sem((NZ,)),
-            sem, sem((NZ // 2,)), sem, sem((NZ,)), sem, sem((NZ,)), sem, sem((NZ,)),
+            sem, sem((NZ,)), sem, sem((NZ,)), sem, sem((NZ,)), sem, sem((NZ,)), sem, sem((NZ,)),
             sem, sem, sem, sem, sem, sem((NZ,)),
             sem, sem, sem, sem, sem, sem,
         ],

time: 51.1 us -> 49.9 us (0.977)
  Pallas kernels: 50.4 us -> 49.1 us
    pallas_call x1, Pallas kernels: 47.2 us -> 45.9 us  [reduced(): pl.pallas_call(functools.partial(reduce_kernel, entries), name='projected...]
where the time goes in v5:
time: 49.9 us; the launch traced here: 49.8 us
  Pallas kernels  49.1 us (98%)
  between operations  0.69 us (1%)
    pallas_call x1, Pallas kernels, reduced(): pl.pallas_call(functools.partial(reduce_kernel, entries), name='projected...  45.9 us
    pallas_call x1, Pallas kernels, updated(): pl.pallas_call(update_kernel, name='adam_update', out_shape=(jax.ShapeDty...  3.17 us

profile of v5, /device:TPU:1, one launch (start us, length us, event | category | flops | bytes accessed | tf_op | source)
XLA Modules:
  0.0 49.8 jit_solution(16894722110102294704)
XLA Ops:
  0.6 0.0 copy-start.2
  0.6 0.0 copy-start.1
  0.7 0.0 copy-start
  0.7 45.9 %projected_gradient.1 = (f32[256,2048]{1,0:T(8,128)S(1)}, f32[8,128]{1,0:T(8,128)S(1)}) custom-call(bf16[512,2048]{1,0:T(8,128)(2,1)} %acts.1, bf16[512,2048]{1,0:T(8,128)(2,1)} %grad.1, bf16[32,256]{1,0:T(8,128)(2,1)} %projector.1), custom_call_target="tpu_custom_call" | custom-call | flops 2147483648 | bytes 6291456 | tf_op jit(solution)/shard_map/projected_gradient/pallas_call | solution.py:336
  46.6 0.0 copy-done.2
  46.6 0.0 copy-done.1
  46.6 0.0 copy-done
  46.6 3.2 %adam_update.1 = (f32[32,2048]{1,0:T(8,128)}, f32[256,2048]{1,0:T(8,128)}, f32[256,2048]{1,0:T(8,128)}) custom-call(f32[256,2048]{1,0:T(8,128)S(1)} %get-tuple-element.5.proj, f32[8,128]{1,0:T(8,128)S(1)} %get-tuple-element.6.clip, bf16[32,256]{1,0:T(8,128)(2,1)S(1)} %copy-done.2, f32[256,2048]{1,0:T(8,128)S(1)} %copy-done, f32[256,2048]{1,0:T(8,128)S(1)} %copy-done.1), custom_call_target="tpu_custom_call" | custom-call | flops 67108864 | bytes 10485760 | tf_op jit(solution)/shard_map/adam_update/pallas_call | solution.py:417
Async XLA Ops:
  0.6 46.0 %copy-start.2 = (bf16[32,256]{1,0:T(8,128)(2,1)S(1)}, bf16[32,256]{1,0:T(8,128)(2,1)}, u32[]{:S(2)}) copy-start(bf16[32,256]{1,0:T(8,128)(2,1)} %projector.1) | copy-start | bytes 49156
  0.6 46.0 %copy-start.1 = (f32[256,2048]{1,0:T(8,128)S(1)}, f32[256,2048]{1,0:T(8,128)}, u32[]{:S(2)}) copy-start(f32[256,2048]{1,0:T(8,128)} %second_old.1) | copy-start | bytes 6291460
  0.7 46.0 %copy-start = (f32[256,2048]{1,0:T(8,128)S(1)}, f32[256,2048]{1,0:T(8,128)}, u32[]{:S(2)}) copy-start(f32[256,2048]{1,0:T(8,128)} %first_old.1) | copy-start | bytes 6291460

commit v6 on v5

--- a/solution.py
+++ b/solution.py
@@ -57,10 +57,10 @@
 def reduce_kernel(
     entries, acts, grad, p_hbm, proj_out, clip_out,
     p_ref, a_all, g_all, p_all, along, lhs, part,
-    yb_send, yb_recv, ys_send, ys_recv, zb_send, zb_recv, column, blocks, scale_all, scale_wide, sums,
+    yb_send, yb_recv, ys_send, ys_recv, zb_send, zb_recv, zs_send, zs_recv, blocks, scales, sums,
     load_sem, pair_send, pair_recv, pz_send, pz_recv, py_send, py_recv,
-    yb_sent, yb_came, ys_sent, ys_came, zb_sent, zb_came, az_sent, az_came, ay_sent, ay_came,
-    sy_sent, sy_came, sc_sent, sc_came, ac_sent, ac_came,
+    yb_sent, yb_came, ys_sent, ys_came, zb_sent, zb_came, zs_sent, zs_came,
+    az_sent, az_came, ay_sent, ay_came, sz_sent, sz_came, sy_sent, sy_came, sc_sent, sc_came, ac_sent, ac_came,
     ex_send, ex_recv, ez_send, ez_recv, ey_send, ey_recv,
 ):
     dp = lax.axis_index("dp")
@@ -72,11 +72,13 @@
     def at(zz, yy, cc, xx):
         return ((zz * NY + yy) * 2 + cc, xx)
 
+    way = 1 - 2 * c
+
     def zoff(d):
-        return lax.rem(z + d, NZ)
+        return lax.rem(z + way * d + NZ, NZ)
 
     def yoff(d):
-        return lax.rem(y + d, NY)
+        return lax.rem(y + way * d + NY, NY)
 
     def xoff(d):
         return lax.rem(x + d, NX)
@@ -126,7 +128,8 @@
     for d in NEAR[1:]:
         for cc in range(2):
             src = p_ref.at[:, pl.ds(cc * 128, 128)]
-            remote(src, p_all.at[mine], pz_send, pz_recv.at[d], at(zoff(d), y, cc, x)).start()
+            seen = jnp.where(c == cc, d, NZ - d)
+            remote(src, p_all.at[mine], pz_send, pz_recv.at[seen], at(zoff(d), y, cc, x)).start()
 
     pair = [
         remote(acts, a_all.at[pl.ds(512, 512)], pair_send.at[0], pair_recv.at[0], sibling),
@@ -173,8 +176,6 @@
     loads[2].wait()
     pair[1].wait_recv()
 
-    row = lax.broadcasted_iota(jnp.int32, (16, 128), 0)
-
     def four_tiles(k, dy):
         return tiles_of(part[k, pl.ds(pl.multiple_of(yoff(dy) * 32, 32), 32), :])
 
@@ -213,44 +214,48 @@
         for i in range(NY - 1):
             total = add(total, [yb_recv[k, i, j] for j in range(4)], ys_recv[k, i])
         if d:
-            message = zb_send.at[d - 1]
             scale = scale_of(total)
             for i, code in enumerate(encode(total, scale)):
-                message[i] = code
-            message[4] = jnp.broadcast_to(scale, (16, 128)).astype(bf16)
-            remote(message, zb_recv.at[d - 1], zb_sent, zb_came.at[d], at(zoff(d), y, c, x)).start()
+                zb_send[d - 1, i] = code
+            zs_send[d - 1] = scale
+            there = at(zoff(d), y, c, x)
+            remote(zb_send.at[d - 1], zb_recv.at[d - 1], zb_sent, zb_came.at[d], there).start()
+            remote(zs_send.at[d - 1], zs_recv.at[d - 1], zs_sent, zs_came.at[d], there).start()
     sent(yb_send, yb_sent)
     sent(ys_send, ys_sent)
     for d in NEAR[1:]:
-        message = zb_recv.at[d - 1]
-        arrived(message, zb_came.at[d])
-        total = add(total, [message[j] for j in range(4)], message[4][:1].astype(f32))
+        arrived(zb_recv.at[d - 1], zb_came.at[d])
+        arrived(zs_recv.at[d - 1], zs_came.at[d])
+        total = add(total, [zb_recv[d - 1, j] for j in range(4)], zs_recv[d - 1])
 
     square = functools.reduce(jnp.add, [t * t for t in total])
     sums[0] = square[:8] + square[8:]
     scale = scale_of(total)
-    packet = column.at[z]
+    mine_out = blocks.at[c, z, y]
     for i, code in enumerate(encode(total, scale)):
-        packet[i] = code
-    packet[4] = jnp.broadcast_to(scale, (16, 128)).astype(bf16)
+        mine_out[i] = code
+    scales[c, y, z] = scale
     for d in (2, 1, 3):
         remote(sums.at[0], sums.at[d], ex_send, ex_recv, at(z, y, c, xoff(d))).start()
     for d in NEAR[1:]:
-        remote(packet, packet, az_sent, az_came.at[d], at(zoff(d), y, c, x)).start()
+        there = at(zoff(d), y, c, x)
+        remote(mine_out, mine_out, az_sent, az_came.at[d], there).start()
+        remote(scales.at[c, y, z], scales.at[c, y, z], sz_sent, sz_came, there).start()
 
     def out_forward(d):
-        zz = zoff(NZ - d)
+        block = blocks.at[c, zoff(NZ - d), y]
         if d:
-            arrived(column.at[zz], az_came.at[d])
-        block = column.at[zz, pl.ds(0, 4)]
+            arrived(block, az_came.at[d])
+        remote(block, block, ac_sent, ac_came.at[d], sibling).start()
         for dy in (2, 1, 3):
-            remote(block, blocks.at[c, zz, y], ay_sent, ay_came.at[d], at(z, yoff(dy), c, x)).start()
-        blocks[c, zz, y] = column[zz, pl.ds(0, 4)]
+            remote(block, block, ay_sent, ay_came.at[d], at(z, yoff(dy), c, x)).start()
 
     def out_share(d):
         block = blocks.at[c, zoff(NZ - d)]
         arrived(blocks.at[c, zoff(NZ - d), pl.ds(0, 3)], ay_came.at[d])
-        remote(block, block, ac_sent, ac_came.at[d], sibling).start()
+        for dy in range(1, NY):
+            piece = blocks.at[c, zoff(NZ - d), yoff(dy)]
+            remote(piece, piece, ac_sent, ac_came.at[d], sibling).start()
 
     for k in range(NZ):
         out_forward(NEAR[k])
@@ -260,11 +265,10 @@
             for d in NEAR[:0:-1]:
                 remote(sums.at[4], sums.at[4 + d], ez_send, ez_recv, at(zoff(d), y, c, x)).start()
 
-    tiles = [column[zz, 4] for zz in range(NZ)]
-    scale_all[c, y] = functools.reduce(lambda a, b: jnp.where(row == b, tiles[b], a), range(1, NZ), tiles[0])
+    arrived(scales.at[c, y, pl.ds(0, 7)], sz_came)
     for dy in (2, 1, 3):
-        block = scale_all.at[c, y]
-        remote(block, block, sy_sent, sy_came, at(z, yoff(dy), c, x)).start()
+        rows = scales.at[c, y]
+        remote(rows, rows, sy_sent, sy_came, at(z, yoff(dy), c, x)).start()
     arrived(sums.at[pl.ds(0, 7)], ez_recv)
     sums[12] = functools.reduce(jnp.add, [sums[i] for i in range(4, 12)])
     slot = 13
@@ -275,14 +279,12 @@
                 remote(sums.at[12], sums.at[slot], ey_send, ey_recv, at(z, yoff(dy), cc, x)).start()
                 slot += 1
     sent(zb_send, zb_sent)
-
-    def widen(cc):
-        scale_wide[cc] = scale_all[cc].astype(f32)
+    sent(zs_send, zs_sent)
 
     def unpack(cc, zz):
         for yy in range(NY):
             codes = [blocks[cc, zz, yy, j] for j in range(4)]
-            for i, t in enumerate(decode(codes, scale_wide[cc, yy, pl.ds(zz, 1), :])):
+            for i, t in enumerate(decode(codes, scales[cc, yy, zz])):
                 rows = pl.ds(pl.multiple_of(cc * 128 + yy * 32 + (i // 2) * 16, 16), 16)
                 cols = pl.ds(pl.multiple_of(zz * 256 + (i % 2) * 128, 128), 128)
                 proj_out[rows, cols] = t
@@ -296,22 +298,18 @@
 
     def unpack_theirs(k, carry):
         d = near(k)
-        zz = zoff(NZ - d)
+        zz = zoff(d)
         arrived(blocks.at[1 - c, zz], ac_came.at[d])
         unpack(1 - c, zz)
         return carry
 
-    for k in range(NZ - 2):
+    for k in range(NZ):
         out_share(NEAR[k])
-    arrived(scale_all.at[c, pl.ds(0, 3)], sy_came)
-    remote(scale_all.at[c], scale_all.at[c], sc_sent, sc_came, sibling).start()
-    widen(c)
-    lax.fori_loop(0, NZ // 2, unpack_own, 0)
-    for k in range(NZ - 2, NZ):
-        out_share(NEAR[k])
-    lax.fori_loop(NZ // 2, NZ, unpack_own, 0)
-    arrived(scale_all.at[1 - c], sc_came)
-    widen(1 - c)
+        if k == 4:
+            arrived(scales.at[c, pl.ds(0, 3)], sy_came)
+            remote(scales.at[c], scales.at[c], sc_sent, sc_came, sibling).start()
+    lax.fori_loop(0, NZ, unpack_own, 0)
+    arrived(scales.at[1 - c], sc_came)
     lax.fori_loop(0, NZ - 2, unpack_theirs, 0)
     arrived(sums.at[pl.ds(0, 7)], ey_recv)
     energy = functools.reduce(jnp.add, [sums[i] for i in range(12, 20)])
@@ -319,10 +317,11 @@
     clip_out[...] = jnp.minimum(1.0, 1.0 / jnp.sqrt(mean))
     lax.fori_loop(NZ - 2, NZ, unpack_theirs, 0)
 
-    sent(column.at[pl.ds(0, 7)], az_sent)
+    sent(zb_send, az_sent)
+    sent(zs_send, sz_sent)
     sent(blocks.at[0, pl.ds(0, 6)], ay_sent)
-    sent(scale_all.at[0, pl.ds(0, 3)], sy_sent)
-    sent(scale_all.at[0], sc_sent)
+    sent(scales.at[0, pl.ds(0, 3)], sy_sent)
+    sent(scales.at[0], sc_sent)
     sent(blocks.at[0], ac_sent)
     sent(sums.at[pl.ds(0, 3)], ex_send)
     sent(sums.at[pl.ds(0, 7)], ez_send)
@@ -351,16 +350,16 @@
             pltpu.VMEM((NZ, NY - 1, 4, 16, 128), bf16),
             pltpu.VMEM((NZ, NY - 1, 1, 128), f32),
             pltpu.VMEM((NZ, NY - 1, 1, 128), f32),
-            pltpu.VMEM((NZ - 1, 5, 16, 128), bf16),
-            pltpu.VMEM((NZ - 1, 5, 16, 128), bf16),
-            pltpu.VMEM((NZ, 5, 16, 128), bf16),
+            pltpu.VMEM((NZ - 1, 4, 16, 128), bf16),
+            pltpu.VMEM((NZ - 1, 4, 16, 128), bf16),
+            pltpu.VMEM((NZ - 1, 1, 128), f32),
+            pltpu.VMEM((NZ - 1, 1, 128), f32),
             pltpu.VMEM((2, NZ, NY, 4, 16, 128), bf16),
-            pltpu.VMEM((2, NY, 16, 128), bf16),
-            pltpu.VMEM((2, NY, 16, 128), f32),
+            pltpu.VMEM((2, NY, NZ, 1, 128), f32),
             pltpu.VMEM((20, 8, 128), f32),
             sem((3,)), sem((2,)), sem((2,)), sem, sem((NZ,)), sem, sem((NZ,)),
-            sem, sem((NZ,)), sem, sem((NZ,)), sem, sem((NZ,)), sem, sem((NZ,)), sem, sem((NZ,)),
-            sem, sem, sem, sem, sem, sem((NZ,)),
+            sem, sem((NZ,)), sem, sem((NZ,)), sem, sem((NZ,)), sem, sem((NZ,)),
+            sem, sem((NZ,)), sem, sem((NZ,)), sem, sem, sem, sem, sem, sem, sem, sem((NZ,)),
             sem, sem, sem, sem, sem, sem,
         ],
         compiler_params=pltpu.CompilerParams(

time: 49.9 us -> 49.6 us (level)
  no operation moved by 1% of the time
where the time goes in v6:
time: 49.6 us; the launch traced here: 49.5 us
  Pallas kernels  48.8 us (98%)
  between operations  0.69 us (1%)
    pallas_call x1, Pallas kernels, reduced(): pl.pallas_call(functools.partial(reduce_kernel, entries), name='projected...  45.7 us
    pallas_call x1, Pallas kernels, updated(): pl.pallas_call(update_kernel, name='adam_update', out_shape=(jax.ShapeDty...  3.17 us

profile of v6, /device:TPU:1, one launch (start us, length us, event | category | flops | bytes accessed | tf_op | source)
XLA Modules:
  0.0 49.5 jit_solution(17299381960958278051)
XLA Ops:
  0.6 0.0 copy-start.2
  0.6 0.0 copy-start.1
  0.7 0.0 copy-start
  0.7 45.7 %projected_gradient.1 = (f32[256,2048]{1,0:T(8,128)S(1)}, f32[8,128]{1,0:T(8,128)S(1)}) custom-call(bf16[512,2048]{1,0:T(8,128)(2,1)} %acts.1, bf16[512,2048]{1,0:T(8,128)(2,1)} %grad.1, bf16[32,256]{1,0:T(8,128)(2,1)} %projector.1), custom_call_target="tpu_custom_call" | custom-call | flops 2147483648 | bytes 6291456 | tf_op jit(solution)/shard_map/projected_gradient/pallas_call | solution.py:335
  46.3 0.0 copy-done.2
  46.3 0.0 copy-done.1
  46.4 0.0 copy-done
  46.4 3.2 %adam_update.1 = (f32[32,2048]{1,0:T(8,128)}, f32[256,2048]{1,0:T(8,128)}, f32[256,2048]{1,0:T(8,128)}) custom-call(f32[256,2048]{1,0:T(8,128)S(1)} %get-tuple-element.5.proj, f32[8,128]{1,0:T(8,128)S(1)} %get-tuple-element.6.clip, bf16[32,256]{1,0:T(8,128)(2,1)S(1)} %copy-done.2, f32[256,2048]{1,0:T(8,128)S(1)} %copy-done, f32[256,2048]{1,0:T(8,128)S(1)} %copy-done.1), custom_call_target="tpu_custom_call" | custom-call | flops 67108864 | bytes 10485760 | tf_op jit(solution)/shard_map/adam_update/pallas_call | solution.py:416
Async XLA Ops:
  0.6 45.7 %copy-start.2 = (bf16[32,256]{1,0:T(8,128)(2,1)S(1)}, bf16[32,256]{1,0:T(8,128)(2,1)}, u32[]{:S(2)}) copy-start(bf16[32,256]{1,0:T(8,128)(2,1)} %projector.1) | copy-start | bytes 49156
  0.6 45.7 %copy-start.1 = (f32[256,2048]{1,0:T(8,128)S(1)}, f32[256,2048]{1,0:T(8,128)}, u32[]{:S(2)}) copy-start(f32[256,2048]{1,0:T(8,128)} %second_old.1) | copy-start | bytes 6291460
  0.7 45.7 %copy-start = (f32[256,2048]{1,0:T(8,128)S(1)}, f32[256,2048]{1,0:T(8,128)}, u32[]{:S(2)}) copy-start(f32[256,2048]{1,0:T(8,128)} %first_old.1) | copy-start | bytes 6291460

commit v7 on v6

--- a/solution.py
+++ b/solution.py
@@ -162,12 +162,10 @@
         else:
             along[...] += term
 
-    lag = 4
-    for k in range(NZ + lag):
-        if k < NZ:
-            p_forward(NEAR[k])
-        if k >= lag:
-            p_use(NEAR[k - lag], k == lag)
+    for d in NEAR:
+        p_forward(d)
+    for d in NEAR:
+        p_use(d, d == 0)
 
     turned = along[...]
     high = turned.astype(bf16)
@@ -186,7 +184,7 @@
 
     multiply(0)
     for k in range(NZ):
-        if k < NZ - 1:
+        if 0 < k < NZ - 1:
             multiply(k + 1)
         for dy in (2, 1, 3):
             tiles = four_tiles(k, dy)
@@ -198,6 +196,8 @@
             there = at(z, yoff(dy), c, x)
             remote(yb_send.at[k, dy - 1], yb_recv.at[k, dy - 1], yb_sent, yb_came.at[k], there).start()
             remote(ys_send.at[k, dy - 1], ys_recv.at[k, dy - 1], ys_sent, ys_came.at[k], there).start()
+        if k == 0:
+            multiply(1)
 
     sent(p_all.at[pl.ds(0, 480)], pz_send)
     sent(p_all.at[pl.ds(0, 1536)], py_send)
@@ -374,7 +374,7 @@
 ):
     scale = clip[:1, :]
     scale = jnp.concatenate([scale, scale], axis=1)
-    rows = projector[...]
+    rows = jnp.concatenate([projector[...], projector[...]], axis=1)
     copies = []
 
     def start(src, dst, i, j):
@@ -383,7 +383,7 @@
         copies[-1].start()
 
     def project(i, high, low):
-        moved = jnp.dot(rows, high, preferred_element_type=f32) + jnp.dot(rows, low, preferred_element_type=f32)
+        moved = jnp.dot(rows, jnp.concatenate([high, low], axis=0), preferred_element_type=f32)
         u_out[:, pl.ds(256 * i, 256)] = galore_scale * moved
 
     waiting = None

time: 49.6 us -> 49.7 us (level)
  no operation moved by 1% of the time
where the time goes in v7:
time: 49.7 us; the launch traced here: 49.6 us
  Pallas kernels  48.9 us (98%)
  between operations  0.69 us (1%)
    pallas_call x1, Pallas kernels, reduced(): pl.pallas_call(functools.partial(reduce_kernel, entries), name='projected...  45.7 us
    pallas_call x1, Pallas kernels, updated(): pl.pallas_call(update_kernel, name='adam_update', out_shape=(jax.ShapeDty...  3.17 us

profile of v7, /device:TPU:1, one launch (start us, length us, event | category | flops | bytes accessed | tf_op | source)
XLA Modules:
  0.0 49.6 jit_solution(3792571413290471381)
XLA Ops:
  0.6 0.0 copy-start.2
  0.6 0.0 copy-start.1
  0.7 0.0 copy-start
  0.7 45.7 %projected_gradient.1 = (f32[256,2048]{1,0:T(8,128)S(1)}, f32[8,128]{1,0:T(8,128)S(1)}) custom-call(bf16[512,2048]{1,0:T(8,128)(2,1)} %acts.1, bf16[512,2048]{1,0:T(8,128)(2,1)} %grad.1, bf16[32,256]{1,0:T(8,128)(2,1)} %projector.1), custom_call_target="tpu_custom_call" | custom-call | flops 2147483648 | bytes 6291456 | tf_op jit(solution)/shard_map/projected_gradient/pallas_call | solution.py:335
  46.4 0.0 copy-done.2
  46.4 0.0 copy-done.1
  46.4 0.0 copy-done
  46.4 3.2 %adam_update.1 = (f32[32,2048]{1,0:T(8,128)}, f32[256,2048]{1,0:T(8,128)}, f32[256,2048]{1,0:T(8,128)}) custom-call(f32[256,2048]{1,0:T(8,128)S(1)} %get-tuple-element.5.proj, f32[8,128]{1,0:T(8,128)S(1)} %get-tuple-element.6.clip, bf16[32,256]{1,0:T(8,128)(2,1)S(1)} %copy-done.2, f32[256,2048]{1,0:T(8,128)S(1)} %copy-done, f32[256,2048]{1,0:T(8,128)S(1)} %copy-done.1), custom_call_target="tpu_custom_call" | custom-call | flops 67108864 | bytes 10485760 | tf_op jit(solution)/shard_map/adam_update/pallas_call | solution.py:416
Async XLA Ops:
  0.6 45.8 %copy-start.2 = (bf16[32,256]{1,0:T(8,128)(2,1)S(1)}, bf16[32,256]{1,0:T(8,128)(2,1)}, u32[]{:S(2)}) copy-start(bf16[32,256]{1,0:T(8,128)(2,1)} %projector.1) | copy-start | bytes 49156
  0.6 45.8 %copy-start.1 = (f32[256,2048]{1,0:T(8,128)S(1)}, f32[256,2048]{1,0:T(8,128)}, u32[]{:S(2)}) copy-start(f32[256,2048]{1,0:T(8,128)} %second_old.1) | copy-start | bytes 6291460
  0.7 45.8 %copy-start = (f32[256,2048]{1,0:T(8,128)S(1)}, f32[256,2048]{1,0:T(8,128)}, u32[]{:S(2)}) copy-start(f32[256,2048]{1,0:T(8,128)} %first_old.1) | copy-start | bytes 6291460

commit v8 on v7

--- a/solution.py
+++ b/solution.py
@@ -228,19 +228,20 @@
         arrived(zs_recv.at[d - 1], zs_came.at[d])
         total = add(total, [zb_recv[d - 1, j] for j in range(4)], zs_recv[d - 1])
 
-    square = functools.reduce(jnp.add, [t * t for t in total])
-    sums[0] = square[:8] + square[8:]
     scale = scale_of(total)
     mine_out = blocks.at[c, z, y]
     for i, code in enumerate(encode(total, scale)):
         mine_out[i] = code
     scales[c, y, z] = scale
-    for d in (2, 1, 3):
-        remote(sums.at[0], sums.at[d], ex_send, ex_recv, at(z, y, c, xoff(d))).start()
     for d in NEAR[1:]:
         there = at(zoff(d), y, c, x)
         remote(mine_out, mine_out, az_sent, az_came.at[d], there).start()
         remote(scales.at[c, y, z], scales.at[c, y, z], sz_sent, sz_came, there).start()
+
+    square = functools.reduce(jnp.add, [t * t for t in total])
+    sums[0] = square[:8] + square[8:]
+    for d in (2, 1, 3):
+        remote(sums.at[0], sums.at[d], ex_send, ex_recv, at(z, y, c, xoff(d))).start()
 
     def out_forward(d):
         block = blocks.at[c, zoff(NZ - d), y]

time: 49.7 us -> 49.8 us (level)
  no operation moved by 1% of the time
where the time goes in v8:
time: 49.8 us; the launch traced here: 49.7 us
  Pallas kernels  49 us (98%)
  between operations  0.69 us (1%)
    pallas_call x1, Pallas kernels, reduced(): pl.pallas_call(functools.partial(reduce_kernel, entries), name='projected...  45.8 us
    pallas_call x1, Pallas kernels, updated(): pl.pallas_call(update_kernel, name='adam_update', out_shape=(jax.ShapeDty...  3.17 us

profile of v8, /device:TPU:1, one launch (start us, length us, event | category | flops | bytes accessed | tf_op | source)
XLA Modules:
  0.0 49.7 jit_solution(3470346767595492563)
XLA Ops:
  0.6 0.0 copy-start.2
  0.6 0.0 copy-start.1
  0.7 0.0 copy-start
  0.7 45.8 %projected_gradient.1 = (f32[256,2048]{1,0:T(8,128)S(1)}, f32[8,128]{1,0:T(8,128)S(1)}) custom-call(bf16[512,2048]{1,0:T(8,128)(2,1)} %acts.1, bf16[512,2048]{1,0:T(8,128)(2,1)} %grad.1, bf16[32,256]{1,0:T(8,128)(2,1)} %projector.1), custom_call_target="tpu_custom_call" | custom-call | flops 2147483648 | bytes 6291456 | tf_op jit(solution)/shard_map/projected_gradient/pallas_call | solution.py:336
  46.5 0.0 copy-done.2
  46.5 0.0 copy-done.1
  46.5 0.0 copy-done
  46.5 3.2 %adam_update.1 = (f32[32,2048]{1,0:T(8,128)}, f32[256,2048]{1,0:T(8,128)}, f32[256,2048]{1,0:T(8,128)}) custom-call(f32[256,2048]{1,0:T(8,128)S(1)} %get-tuple-element.5.proj, f32[8,128]{1,0:T(8,128)S(1)} %get-tuple-element.6.clip, bf16[32,256]{1,0:T(8,128)(2,1)S(1)} %copy-done.2, f32[256,2048]{1,0:T(8,128)S(1)} %copy-done, f32[256,2048]{1,0:T(8,128)S(1)} %copy-done.1), custom_call_target="tpu_custom_call" | custom-call | flops 67108864 | bytes 10485760 | tf_op jit(solution)/shard_map/adam_update/pallas_call | solution.py:417
Async XLA Ops:
  0.6 45.9 %copy-start.2 = (bf16[32,256]{1,0:T(8,128)(2,1)S(1)}, bf16[32,256]{1,0:T(8,128)(2,1)}, u32[]{:S(2)}) copy-start(bf16[32,256]{1,0:T(8,128)(2,1)} %projector.1) | copy-start | bytes 49156
  0.6 45.9 %copy-start.1 = (f32[256,2048]{1,0:T(8,128)S(1)}, f32[256,2048]{1,0:T(8,128)}, u32[]{:S(2)}) copy-start(f32[256,2048]{1,0:T(8,128)} %second_old.1) | copy-start | bytes 6291460
  0.7 45.9 %copy-start = (f32[256,2048]{1,0:T(8,128)S(1)}, f32[256,2048]{1,0:T(8,128)}, u32[]{:S(2)}) copy-start(f32[256,2048]{1,0:T(8,128)} %first_old.1) | copy-start | bytes 6291460
